TPU v7x, 32 devices: a whole 2x2x4 slice. The times are simulated.
32 devices in a mesh: blk: 8 (over z, x), uly: 4 (over y, core).
Axes of the slice: x: 2, y: 2, z: 4, core: 2. Of those that a mesh axis runs over, the one named last changes fastest.
Arguments:
- tokens: bfloat16 [768, 2560], P(('blk', 'uly')), may hold values from -6 to 6
- in_bits: int32 [768, 2560], P(('blk', 'uly')), may hold values from 0 to 1
- qkv_weights: bfloat16 [2, 3, 2560, 2560], P(None, None, 'blk', 'uly'), may hold values from -0.125 to 0.125
- qkv_bits: int32 [768, 3, 2560], P('blk', None, 'uly'), may hold values from 0 to 1
- gain_query: float32 [2560], P('uly'), may hold values from 0.7 to 1.8
- gain_key: float32 [2560], P('uly'), may hold values from 0.7 to 1.8
- out_weights: bfloat16 [2, 2560, 2560], P(None, 'uly', 'blk'), may hold values from -0.5 to 0.5
- mix_bits: int32 [768, 2560], P('blk', 'uly'), may hold values from 0 to 1
- out_bits: int32 [768, 2560], P('blk'), may hold values from 0 to 1
Outputs:
- layer_output: bfloat16 [768, 2560], P(('blk', 'uly'))
Inputs may be any that keep to these rules, and one draw needn't show every extreme that they name: `in_bits`: a bit of 1 stands for the sign +1, a bit of 0 for -1. `qkv_bits`: a bit of 1 stands for the sign +1, a bit of 0 for -1. `mix_bits`: a bit of 1 stands for the sign +1, a bit of 0 for -1. `out_bits`: a bit of 1 stands for the sign +1, a bit of 0 for -1.
All inputs are finite; a program needn't handle non-finite values.
Results may differ from a plain program's by a relative error of at most 0.018.
Values may be sent and summed in bfloat16 or wider, within the bound.
No kernel may reach another device: no remote copies, remote signals or barrier semaphores. Data moves between devices by JAX's collectives and lax.ppermute only.
A program may use at most 128 MiB of HBM per device.

v0:
```python
import math

import jax
import jax.numpy as jnp
from jax import lax
from jax.sharding import PartitionSpec as P

HEAD = 128


epsilon = 1e-06


def signed(bit_values):
    return (2 * bit_values - 1).astype(jnp.float32)


def normalize(values, gain_vector):
    row_count = values.shape[0]
    by_head = values.astype(jnp.float32).reshape(row_count, -1, HEAD)
    inverse_rms = lax.rsqrt(jnp.mean(by_head * by_head, axis=-1, keepdims=True) + epsilon)
    return (by_head * inverse_rms * gain_vector.reshape(-1, HEAD)).astype(jnp.bfloat16)


def body(
    tokens, in_bits, qkv_weights, qkv_bits, gain_query, gain_key, out_weights, mix_bits, out_bits
):
    flipped = (tokens.astype(jnp.float32) * signed(in_bits)).astype(jnp.bfloat16)
    group_rows = lax.all_gather(jnp.stack([tokens, flipped]), "uly", axis=1, tiled=True)
    row_total = group_rows.shape[1]
    projections = jnp.einsum(
        "mrd,mkdc->rmkc",
        group_rows,
        lax.all_gather(qkv_weights, "blk", axis=2, tiled=True),
        preferred_element_type=jnp.float32,
    )
    projected = (projections[:, 0] + signed(qkv_bits) * projections[:, 1]).astype(jnp.bfloat16)
    queries = normalize(projected[:, 0], gain_query)
    head_count = queries.shape[1]
    keys_normed = normalize(projected[:, 1], gain_key).reshape(row_total, -1)
    values_block = projected[:, 2]
    score_scale = 1.0 / math.sqrt(HEAD)

    def attend(running, shard_piece):
        numerator, denominator = running
        key_rows = shard_piece[0].reshape(shard_piece[0].shape[0], head_count, HEAD)
        value_rows = shard_piece[1].reshape(shard_piece[1].shape[0], head_count, HEAD)
        scores = (
            jnp.einsum("rhd,nhd->hrn", queries, key_rows, preferred_element_type=jnp.float32)
            * score_scale
        )
        weights = jnp.exp(scores).astype(jnp.bfloat16)
        numerator = numerator + jnp.einsum(
            "hrn,nhd->rhd", weights, value_rows, preferred_element_type=jnp.float32
        )
        denominator = denominator + jnp.sum(weights.astype(jnp.float32), axis=2).T
        return (numerator, denominator)

    start_state = (
        jnp.zeros((row_total, head_count, HEAD), jnp.float32),
        jnp.zeros((row_total, head_count), jnp.float32),
    )
    all_keys, all_values = (
        lax.all_gather(keys_normed, "blk", axis=0, tiled=True),
        lax.all_gather(values_block, "blk", axis=0, tiled=True),
    )
    group_count = lax.axis_size("blk")
    per_block = 1
    while per_block * row_total < 512 and group_count % (per_block * 2) == 0:
        per_block = per_block * 2
    block_rows = per_block * row_total
    block_count = group_count // per_block
    key_blocks = all_keys.reshape(block_count, block_rows, all_keys.shape[1])
    value_blocks = all_values.reshape(block_count, block_rows, all_values.shape[1])

    def scan_step(running, block_pair):
        return (attend(running, block_pair), None)

    (numerator, denominator), unused = lax.scan(scan_step, start_state, (key_blocks, value_blocks))
    attended = (numerator / denominator[:, :, None]).astype(jnp.bfloat16).reshape(row_total, -1)
    attended_flipped = (attended.astype(jnp.float32) * signed(mix_bits)).astype(jnp.bfloat16)
    attended_pair = jnp.stack([attended, attended_flipped])
    out_signs = signed(out_bits)
    partial_out = jnp.einsum(
        "mrc,mcn->rmn",
        attended_pair,
        lax.all_gather(out_weights, "blk", axis=2, tiled=True),
        preferred_element_type=jnp.float32,
    )
    summed = lax.psum_scatter(
        partial_out.astype(jnp.bfloat16), "uly", scatter_dimension=0, tiled=True
    ).astype(jnp.float32)
    own_rows = summed.shape[0]
    own_signs = lax.dynamic_slice_in_dim(out_signs, lax.axis_index("uly") * own_rows, own_rows, 0)
    result_rows = summed[:, 0] + own_signs * summed[:, 1]
    return result_rows.astype(jnp.bfloat16)


def solution(mesh):
    return jax.shard_map(
        body,
        mesh=mesh,
        in_specs=(
            P(("blk", "uly"), None),
            P(("blk", "uly"), None),
            P(None, None, "blk", "uly"),
            P("blk", None, "uly"),
            P("uly"),
            P("uly"),
            P(None, "uly", "blk"),
            P("blk", "uly"),
            P("blk", None),
        ),
        out_specs=P(("blk", "uly"), None),
        check_vma=False,
    )
```

profile of v0, /device:TPU:0, one launch (start us, length us, event | category | flops | bytes accessed | tf_op | source)
XLA Modules:
  0.0 553.8 jit_solution(6988524084516603778)
XLA Ops:
  6.5 0.0 copy-start.2
  6.5 0.0 copy-start.1
  6.5 0.0 all-gather.4.cloned.1.call-start
  6.5 0.7 all-gather.4.cloned.1.call-update
  7.3 0.0 all-gather.6.cloned.1.call-start
  7.3 0.7 all-gather.6.cloned.1.call-update
  8.0 0.0 reduce-scatter.4.cloned.1.call-start
  8.1 0.0 copy-done.2
  8.1 0.0 copy-done.1
  8.1 0.1 fusion.20
  8.2 11.1 %all_gather.15 = bf16[2,96,2560]{2,1,0:T(8,128)(2,1)S(1)} all-gather(bf16[2,24,2560]{2,1,0:T(8,128)(2,1)S(1)} %pad_maximum_fusion), channel_id=1, replica_groups=mesh['blk'=8,'uly'=4] {'uly'}, dimensions={1}, use_global_device_ids=true | all-gather | bytes 1228800 | tf_op jit(solution)/shard_map/all_gather | solution.py:29
  19.3 0.0 copy-start
  19.3 369.5 %all-gather.4.cloned.1.call-done = bf16[2,3,2560,640]{3,2,1,0:T(8,128)(2,1)} async-done(((bf16[2,3,320,640]{3,2,1,0:T(8,128)(2,1)}), bf16[2,3,2560,640]{3,2,1,0:T(8,128)(2,1)}) %all-gather.4.cloned.1.call-update) | async-done | bytes 19660816 | tf_op jit(solution)/shard_map/all_gather | solution.py:34
  388.8 8.3 %convolution_bitcast_fusion = f32[96,2,3,640]{3,0,2,1:T(8,128)S(1)} fusion(bf16[2,3,2560,640]{3,2,1,0:T(8,128)(2,1)} %all-gather.4.cloned.1.call-done, bf16[2,96,2560]{2,1,0:T(8,128)(2,1)S(1)} %all_gather.15), kind=kOutput, calls=%fused_computation.4 | convolution fusion | flops 1887436800 | bytes 22118400 | tf_op jit(solution)/shard_map/mrd,mkdc->rmkc/dot_general | solution.py:31
  397.1 0.0 copy-done
  397.1 0.0 copy-start.4
  397.2 0.2 fusion.6
  397.4 0.2 copy.28
  397.6 0.2 copy.29
  397.8 0.1 copy-done.4
  397.9 35.6 %all_gather.18 = bf16[768,640]{1,0:T(8,128)(2,1)S(1)} all-gather(bf16[96,640]{1,0:T(8,128)(2,1)S(1)} %fusion.9), channel_id=1, replica_groups=mesh['blk'=8,'uly'=4] {'blk'}, dimensions={0}, use_global_device_ids=true | all-gather | bytes 1105920 | tf_op jit(solution)/shard_map/all_gather | solution.py:64
  433.5 0.6 copy.30
  434.2 0.0 copy-start.5
  434.2 0.2 copy.27
  434.4 35.2 %all-gather = bf16[768,1,640]{2,0,1:T(8,128)(2,1)S(1)} all-gather(bf16[96,1,640]{2,0,1:T(8,128)(2,1)S(1)} %get-tuple-element.16), channel_id=2, replica_groups=mesh['blk'=8,'uly'=4] {'blk'}, dimensions={0}, use_global_device_ids=true | all-gather | bytes 1105920 | tf_op jit(solution)/shard_map/all_gather | solution.py:65
  469.6 0.6 copy.26
  470.3 0.0 copy-done.5
  470.3 0.7 convert_reduce_fusion
  471.0 0.0 copy-start.3
  471.0 0.4 fusion.2
  471.5 0.1 copy.35
  471.6 0.2 copy.34
  471.8 0.2 copy.36
  471.9 0.2 copy.37
  472.1 0.0 copy-done.3
  472.2 42.0 %all-gather.6.cloned.1.call-done = bf16[2,640,2560]{1,2,0:T(8,128)(2,1)} async-done(((bf16[2,640,320]{1,2,0:T(8,128)(2,1)}), bf16[2,640,2560]{1,2,0:T(8,128)(2,1)}) %all-gather.6.cloned.1.call-update) | async-done | bytes 6553616 | tf_op jit(solution)/shard_map/all_gather | solution.py:87
  514.2 5.0 fusion
  519.1 1.0 copy.45
  520.2 0.0 reduce-scatter.4.cloned.1.call-update
  520.2 24.5 %reduce-scatter.4.cloned.1.call-done = bf16[24,5120]{1,0:T(8,128)(2,1)} async-done(((bf16[96,5120]{1,0:T(8,128)(2,1)}), bf16[24,5120]{1,0:T(8,128)(2,1)}) %reduce-scatter.4.cloned.1.call-update) | async-done | bytes 245776
  544.7 1.0 bitcast_convert_fusion
  545.6 1.7 fusion.12
  (10 shorter events, 0.3 us)
Async XLA Ops:
  6.5 1.5 copy-start.2
  6.5 1.5 copy-start.1
  6.5 382.3 %all-gather.4.cloned.1.call-start = ((), (), s32[]{:S(2)}) async-start(), calls=%async_computation.1 | async-start | bytes 22118400 | tf_op jit(solution)/shard_map/all_gather | solution.py:34
  7.3 506.9 %all-gather.6.cloned.1.call-start = ((), (), s32[]{:S(2)}) async-start(), calls=%async_computation.2 | async-start | bytes 7372800 | tf_op jit(solution)/shard_map/all_gather | solution.py:87
  8.0 536.7 %reduce-scatter.4.cloned.1.call-start = ((), (), s32[]{:S(2)}) async-start(), calls=%async_computation.3 | async-start | bytes 1228800
  19.3 377.8 %copy-start = (s32[96,3,640]{2,0,1:T(8,128)S(1)}, s32[96,3,640]{2,0,1:T(8,128)}, u32[]{:S(2)}) copy-start(s32[96,3,640]{2,0,1:T(8,128)} %param.12) | copy-start | bytes 2211844
  397.1 0.7 copy-start.4
  434.2 36.2 %copy-start.5 = (f32[640]{0:T(1024)S(1)}, f32[640]{0:T(1024)}, u32[]{:S(2)}) copy-start(f32[640]{0:T(1024)} %param.13) | copy-start | bytes 7684
  471.0 1.1 copy-start.3
Sparse Core Ops, SparseCore 0:
  8.9 379.8 all-gather.3
  391.0 123.0 all-gather.5
  520.3 24.3 reduce-scatter.3
where the time goes:
time: 554 us
  waiting for transfers between devices  437 us (79%)
  blocking collectives  82 us (15%)
  matrix products  14.4 us (3%)
  between operations  13.3 us (2%)
    all_gather x1, waiting for transfers between devices, body(): lax.all_gather(qkv_weights, 'blk', axis=2, tiled=True)  370 us
    all_gather x1, waiting for transfers between devices, body(): lax.all_gather(out_weights, 'blk', axis=2, tiled=True)  42 us
    all_gather x1, blocking collectives, body(): lax.all_gather(keys_normed, 'blk', axis=0, tiled=True)  35.6 us
    all_gather x1, blocking collectives, body(): lax.all_gather(values_block, 'blk', axis=0, tiled=True)  35.2 us
    unnamed x4, waiting for transfers between devices  25.9 us
    all_gather x1, blocking collectives, body(): lax.all_gather(jnp.stack([tokens, flipped]), 'uly', axis=1, tiled=True)  11.1 us
  transfers between devices with their start and end apart: 3, of which 3 were waited for; matrix products, arithmetic and copies ran while one was open for 2% of the time, Pallas kernels for 0%

commit v1 on v0

--- a/solution.py
+++ b/solution.py
@@ -22,7 +22,7 @@
     return (by_head * inverse_rms * gain_vector.reshape(-1, HEAD)).astype(jnp.bfloat16)
 
 
-def body(
+def gather_plan(
     tokens, in_bits, qkv_weights, qkv_bits, gain_query, gain_key, out_weights, mix_bits, out_bits
 ):
     flipped = (tokens.astype(jnp.float32) * signed(in_bits)).astype(jnp.bfloat16)
@@ -94,6 +94,190 @@
     own_signs = lax.dynamic_slice_in_dim(out_signs, lax.axis_index("uly") * own_rows, own_rows, 0)
     result_rows = summed[:, 0] + own_signs * summed[:, 1]
     return result_rows.astype(jnp.bfloat16)
+
+
+def dot32(a, b):
+    return lax.dot_general(
+        a, b, (((1,), (0,)), ((), ())), preferred_element_type=jnp.float32
+    )
+
+
+def dot32_t(a, b):
+    return lax.dot_general(
+        a, b, (((1,), (1,)), ((), ())), preferred_element_type=jnp.float32
+    )
+
+
+def norm_rows(values, gain_row):
+    wide = values.astype(jnp.float32)
+    inverse_rms = lax.rsqrt(jnp.mean(wide * wide, axis=-1, keepdims=True) + epsilon)
+    return (wide * inverse_rms * gain_row).astype(jnp.bfloat16)
+
+
+def attend(queries, keys, values):
+    scores = dot32_t(queries, keys) * (1.0 / math.sqrt(HEAD))
+    weights = jnp.exp(scores).astype(jnp.bfloat16)
+    totals = jnp.sum(weights.astype(jnp.float32), axis=1, keepdims=True)
+    return (dot32(weights, values) / totals).astype(jnp.bfloat16)
+
+
+def stationary_plan(
+    tokens, in_bits, qkv_weights, qkv_bits, gain_query, gain_key, out_weights, mix_bits, out_bits
+):
+    groups = lax.axis_size("blk")
+    team = lax.axis_size("uly")
+    depth = groups // 2
+    z = lax.axis_index("blk") // 2
+    x = lax.axis_index("blk") % 2
+    u = lax.axis_index("uly")
+    own_rows, width = tokens.shape
+    slab = qkv_weights.shape[2]
+    columns = qkv_weights.shape[3]
+    group_rows = own_rows * team
+    heads = columns // HEAD
+    half_rows = depth * group_rows
+
+    def swap_x(value):
+        return lax.ppermute(value, "blk", [(i, i ^ 1) for i in range(groups)])
+
+    def swap_z(value, step):
+        return lax.ppermute(value, "blk", [(i, i ^ (2 * step)) for i in range(groups)])
+
+    def swap_u(value, bit):
+        return lax.ppermute(value, "uly", [(i, i ^ bit) for i in range(team)])
+
+    bf = jnp.bfloat16
+    steps = range(depth)
+
+    flipped = (tokens.astype(jnp.float32) * signed(in_bits)).astype(bf)
+    pair = jnp.stack([tokens, flipped])
+
+    def feature_block(target):
+        first = lax.dynamic_slice_in_dim(pair, (2 * target + x) * slab, slab, 2)
+        second = lax.dynamic_slice_in_dim(pair, (2 * target + 1 - x) * slab, slab, 2)
+        return jnp.concatenate([first, second], axis=2)
+
+    pieces = [feature_block(z)] + [swap_z(feature_block(z ^ k), k) for k in steps if k]
+    held = jnp.stack(pieces, axis=1)
+    held = lax.all_gather(held, "uly", axis=2, tiled=False)
+    rows = held.reshape(2, half_rows, 2 * slab)
+
+    signs_own = jnp.transpose(2 * qkv_bits - 1, (1, 0, 2)).astype(bf)
+    signs = {}
+    partner = {}
+    for part in (2, 1, 0):
+        signs[part] = jnp.concatenate(
+            [signs_own[part]] + [swap_z(signs_own[part], k) for k in steps if k], axis=0
+        )
+        partner[part] = swap_x(qkv_weights[:, part])
+
+    out_t = jnp.transpose(out_weights, (0, 2, 1))
+    out_partner = swap_x(out_t)
+    mix_own = (2 * mix_bits - 1).astype(bf)
+    mix_all = [mix_own] + [swap_z(mix_own, k) for k in steps if k]
+
+    whole_heads = heads // depth
+    rest = heads - whole_heads * depth
+    assert whole_heads == 1 and rest == 1
+
+    def head_of(value, index):
+        return lax.dynamic_slice_in_dim(value, index * HEAD, HEAD, 1)
+
+    def project(part):
+        total = [
+            dot32(rows[m, :, :slab], qkv_weights[m, part])
+            + dot32(rows[m, :, slab:], partner[part][m])
+            for m in (0, 1)
+        ]
+        partial = (total[0] + signs[part].astype(jnp.float32) * total[1]).astype(bf)
+        shared = partial[:, depth * HEAD :]
+        got_main, got_rest = [], []
+        for k in steps:
+            block = jnp.concatenate(
+                [
+                    head_of(partial, z ^ k),
+                    shared[k * group_rows : (k + 1) * group_rows],
+                ],
+                axis=0,
+            )
+            if k:
+                block = swap_z(block, k)
+            main = block[:half_rows].reshape(depth, group_rows, HEAD)
+            got_main.append(jnp.stack([main[j ^ k] for j in steps]))
+            got_rest.append(block[half_rows:])
+        main = sum(g.astype(jnp.float32) for g in got_main).reshape(half_rows, HEAD)
+        other = sum(g.astype(jnp.float32) for g in got_rest)
+        return main.astype(bf), other.astype(bf)
+
+    gain_q = gain_query.reshape(heads, HEAD)
+    gain_k = gain_key.reshape(heads, HEAD)
+
+    def gains(table):
+        return lax.dynamic_slice_in_dim(table, z, 1, 0), table[depth : depth + 1]
+
+    def spread(main, other):
+        both = jnp.concatenate([main, swap_x(main)], axis=0)
+        line = jnp.concatenate([other] + [swap_z(other, k) for k in steps if k], axis=0)
+        return both, jnp.concatenate([line, swap_x(line)], axis=0)
+
+    value_main, value_rest = spread(*project(2))
+    key_main, key_rest = project(1)
+    gain_main, gain_rest = gains(gain_k)
+    key_main, key_rest = spread(norm_rows(key_main, gain_main), norm_rows(key_rest, gain_rest))
+    query_main, query_rest = project(0)
+    gain_main, gain_rest = gains(gain_q)
+    query_main, query_rest = norm_rows(query_main, gain_main), norm_rows(query_rest, gain_rest)
+
+    done_main = attend(query_main, key_main, value_main)
+    done_rest = attend(query_rest, key_rest, value_rest)
+    done = jnp.concatenate([done_main, done_rest], axis=0)
+
+    by_head, last_head = [], []
+    for k in steps:
+        block = swap_z(done, k) if k else done
+        main = block[:half_rows].reshape(depth, group_rows, HEAD)
+        by_head.append(jnp.concatenate([main[j ^ k] for j in steps], axis=0))
+        last_head.append(block[half_rows:])
+    attended = jnp.concatenate(by_head + [jnp.concatenate(last_head, axis=0)], axis=1)
+
+    def relative(value, axis):
+        parts = [
+            lax.dynamic_slice_in_dim(value, (z ^ k) * HEAD, HEAD, axis) for k in steps
+        ] + [lax.slice_in_dim(value, depth * HEAD, heads * HEAD, axis=axis)]
+        return jnp.concatenate(parts, axis=axis)
+
+    mix = relative(jnp.concatenate(mix_all, axis=0), 1)
+    attended_flipped = attended * mix
+    first = jnp.where(x == 0, out_t, out_partner)
+    second = jnp.where(x == 0, out_partner, out_t)
+    out_full = relative(jnp.concatenate([first, second], axis=1), 2)
+    partial = jnp.stack(
+        [dot32_t(attended, out_full[0]), dot32_t(attended_flipped, out_full[1])]
+    ).astype(bf)
+    partial = partial.reshape(2, depth, 2, 2, own_rows, 2 * slab)
+    core = u % 2
+    y = u // 2
+    keep = lax.dynamic_index_in_dim(partial, core, 3, keepdims=False)
+    send = lax.dynamic_index_in_dim(partial, 1 - core, 3, keepdims=False)
+    summed = keep.astype(jnp.float32) + swap_u(send, 1).astype(jnp.float32)
+    keep = lax.dynamic_index_in_dim(summed, y, 2, keepdims=False)
+    send = lax.dynamic_index_in_dim(summed, 1 - y, 2, keepdims=False).astype(bf)
+    summed = (keep + swap_u(send, 2).astype(jnp.float32)).astype(bf)
+    final = [summed[:, 0]] + [swap_z(summed[:, k], k) for k in steps if k]
+    placed = jnp.zeros((2, own_rows, depth, 2 * slab), bf)
+    for k in steps:
+        placed = lax.dynamic_update_slice_in_dim(placed, final[k][:, :, None], z ^ k, 2)
+    placed = placed.reshape(2, own_rows, width).astype(jnp.float32)
+    own_bits = lax.dynamic_slice_in_dim(out_bits, u * own_rows, own_rows, 0)
+    return (placed[0] + signed(own_bits) * placed[1]).astype(bf)
+
+
+def body(*arrays):
+    heads = arrays[2].shape[3] // HEAD
+    depth = lax.axis_size("blk") // 2
+    if depth == heads - 1 and depth & (depth - 1) == 0 and lax.axis_size("uly") == 4:
+        return stationary_plan(*arrays)
+    return gather_plan(*arrays)
 
 
 def solution(mesh):

time: 554 us -> 200 us (0.36)
  waiting for transfers between devices: 437 us -> 76.5 us
  blocking collectives: 82 us -> 9.7 us
  starting transfers between devices: 0.08 us -> 68.5 us
  other arithmetic: 3.12 us -> 21.3 us
  between operations: 13.3 us -> 0.94 us
  local copies, waits for them, and re-layouts: 3.55 us -> 13.3 us
    all_gather x2 -> x0, waiting for transfers between devices: 412 us -> none  [the longest x1 370 us: body(): lax.all_gather(qkv_weights, 'blk', axis=2, tiled=True)]
    ppermute x0 -> x46, waiting for transfers between devices: none -> 76.5 us  [the longest x8 49.4 us: swap_x(): return lax.ppermute(value, 'blk', [(i, i ^ 1) for i in range(groups)])]
    all_gather x3 -> x1, blocking collectives: 82 us -> 9.7 us  [stationary_plan(): held = lax.all_gather(held, 'uly', axis=2, tiled=False)]
    ppermute x0 -> x46, starting transfers between devices: none -> 68.5 us  [the longest x36 58.7 us: swap_z(): lax.ppermute(value, 'blk', [(i, i ^ 2 * step) for i in range(groups)])]
    unnamed x4 -> x0, waiting for transfers between devices: 25.9 us -> none
    dot_general x4 -> x18, matrix products: 14.4 us -> 9.33 us  [the longest x14 7.15 us: dot32(): lax.dot_general(a, b, (((1,), (0,)), ((), ())), preferred_element_type=jn...]
  transfers between devices with their start and end apart: 3 -> 46, of which waited for: 3 -> 13; matrix products, arithmetic and copies ran while one was open for 2% -> 18% of each run, Pallas kernels for 0% -> 0%
where the time goes in v1:
time: 200 us
  waiting for transfers between devices  76.5 us (38%)
  starting transfers between devices  68.5 us (34%)
  other arithmetic  21.3 us (11%)
  local copies, waits for them, and re-layouts  13.3 us (7%)
  blocking collectives  9.7 us (5%)
  matrix products  9.33 us (5%)
    ppermute x36, starting transfers between devices, swap_z(): lax.ppermute(value, 'blk', [(i, i ^ 2 * step) for i in range(groups)])  58.7 us
    ppermute x8, waiting for transfers between devices, swap_x(): return lax.ppermute(value, 'blk', [(i, i ^ 1) for i in range(groups)])  49.4 us
    ppermute x36, waiting for transfers between devices, swap_z(): lax.ppermute(value, 'blk', [(i, i ^ 2 * step) for i in range(groups)])  17.7 us
    all_gather x1, blocking collectives, stationary_plan(): held = lax.all_gather(held, 'uly', axis=2, tiled=False)  9.7 us
    ppermute x2, waiting for transfers between devices, swap_u(): return lax.ppermute(value, 'uly', [(i, i ^ bit) for i in range(team)])  9.33 us
    ppermute x8, starting transfers between devices, swap_x(): return lax.ppermute(value, 'blk', [(i, i ^ 1) for i in range(groups)])  9.21 us
    dot_general x14, matrix products, dot32(): lax.dot_general(a, b, (((1,), (0,)), ((), ())), preferred_element_type=jn...  7.15 us
  transfers between devices with their start and end apart: 46, of which 13 were waited for; matrix products, arithmetic and copies ran while one was open for 18% of the time, Pallas kernels for 0%

profile of v1, /device:TPU:0, one launch (start us, length us, event | category | flops | bytes accessed | tf_op | source)
XLA Modules:
  0.0 199.6 jit_solution(16807448578776075378)
XLA Ops:
  0.0 1.4 fusion.38
  2.0 3.0 %collective-permute-start.19 = (bf16[96,640]{1,0:T(8,128)(2,1)}, bf16[96,640]{1,0:T(8,128)(2,1)}, u32[]{:S(2)}, u32[]{:S(2)}) collective-permute-start(bf16[96,640]{1,0:T(8,128)(2,1)} %get-tuple-element.57), channel_id=1, source_target_pairs={{0,8},{4,12},{8,0},{12,4},{16,24},{20,28},{24,16},{28,20},{1,9},{5... | collective-permute-start | bytes 368648 | tf_op jit(solution)/shard_map/ppermute | solution.py:144
  5.1 2.6 %collective-permute-start.20 = (bf16[96,640]{1,0:T(8,128)(2,1)}, bf16[96,640]{1,0:T(8,128)(2,1)}, u32[]{:S(2)}, u32[]{:S(2)}) collective-permute-start(bf16[96,640]{1,0:T(8,128)(2,1)} %get-tuple-element.57), channel_id=1, source_target_pairs={{0,16},{4,20},{8,24},{12,28},{16,0},{20,4},{24,8},{28,12},{1,17},{... | collective-permute-start | bytes 368648 | tf_op jit(solution)/shard_map/ppermute | solution.py:144
  11.1 3.9 %collective-permute-start.2 = (bf16[2,24,640]{2,1,0:T(8,128)(2,1)}, bf16[2,24,640]{2,1,0:T(8,128)(2,1)}, u32[]{:S(2)}, u32[]{:S(2)}) collective-permute-start(bf16[2,24,640]{2,1,0:T(8,128)(2,1)} %pad_maximum_fusion.21), channel_id=1, source_target_pairs={{0,24},{4,28},{8,16},{12,20},{16,8},{20,12},{24,0},{28,4},{1,25},{... | collective-permute-start | bytes 184328 | tf_op jit(solution)/shard_map/ppermute | solution.py:144
  15.1 1.4 slice_bitcast_fusion.4
  17.7 1.3 slice.744
  18.9 1.6 add_convert_fusion.2
  20.5 1.5 maximum_bitcast_fusion
  22.0 1.3 fusion.81
  25.1 3.8 %collective-permute-start.40 = (bf16[96,640]{1,0:T(8,128)(2,1)}, bf16[96,640]{1,0:T(8,128)(2,1)S(1)}, u32[]{:S(2)}, u32[]{:S(2)}) collective-permute-start(bf16[96,640]{1,0:T(8,128)(2,1)} %add_convert_fusion.2), channel_id=1, source_target_pairs={{0,24},{4,28},{8,16},{12,20},{16,8},{20,12},{24,0},{28,4},{1,25},{... | collective-permute-start | bytes 368648 | tf_op jit(solution)/shard_map/ppermute | solution.py:144
  29.8 9.7 %all-gather = bf16[2,4,96,640]{3,2,1,0:T(8,128)(2,1)S(1)} all-gather(bf16[2,4,24,640]{3,2,1,0:T(8,128)(2,1)S(1)} %pad_maximum_fusion.2), channel_id=2, replica_groups=mesh['blk'=8,'uly'=4] {'uly'}, dimensions={2}, use_global_device_ids=true | all-gather | bytes 1228800 | tf_op jit(solution)/shard_map/all_gather | solution.py:162
  42.5 1.5 collective-permute-start.18
  44.8 18.7 %collective-permute-done.18 = bf16[2,320,640]{2,1,0:T(8,128)(2,1)S(1)} collective-permute-done((bf16[2,320,640]{2,1,0:T(8,128)(2,1)S(1)}, bf16[2,320,640]{2,1,0:T(8,128)(2,1)S(1)}, u32[]{:S(2)}, u32[]{:S(2)}) %collective-permute-start.18) | collective-permute-done | bytes 819232 | tf_op jit(solution)/shard_map/ppermute | solution.py:141
  64.1 4.3 %collective-permute-start.5 = (bf16[96,640]{1,0:T(8,128)(2,1)S(1)}, bf16[96,640]{1,0:T(8,128)(2,1)S(1)}, u32[]{:S(2)}, u32[]{:S(2)}) collective-permute-start(bf16[96,640]{1,0:T(8,128)(2,1)S(1)} %get-tuple-element.59), channel_id=1, source_target_pairs={{0,16},{4,20},{8,24},{12,28},{16,0},{20,4},{24,8},{28,12},{1,17},{... | collective-permute-start | bytes 368648 | tf_op jit(solution)/shard_map/ppermute | solution.py:144
  68.5 1.5 collective-permute-start.10
  70.0 1.5 fusion.7
  71.6 9.5 %collective-permute-done.3 = bf16[2,320,640]{2,1,0:T(8,128)(2,1)S(1)} collective-permute-done((bf16[2,320,640]{2,1,0:T(8,128)(2,1)S(1)}, bf16[2,320,640]{2,1,0:T(8,128)(2,1)S(1)}, u32[]{:S(2)}, u32[]{:S(2)}) %collective-permute-start.3) | collective-permute-done | bytes 819232 | tf_op jit(solution)/shard_map/ppermute | solution.py:141
  81.6 16.4 %collective-permute-done.10 = bf16[2,320,640]{2,1,0:T(8,128)(2,1)S(1)} collective-permute-done((bf16[2,320,640]{2,1,0:T(8,128)(2,1)S(1)}, bf16[2,320,640]{2,1,0:T(8,128)(2,1)S(1)}, u32[]{:S(2)}, u32[]{:S(2)}) %collective-permute-start.10) | collective-permute-done | bytes 819232 | tf_op jit(solution)/shard_map/ppermute | solution.py:141
  98.8 3.3 %collective-permute-start.13 = (bf16[96,640]{1,0:T(8,128)(2,1)S(1)}, bf16[96,640]{1,0:T(8,128)(2,1)S(1)}, u32[]{:S(2)}, u32[]{:S(2)}) collective-permute-start(bf16[96,640]{1,0:T(8,128)(2,1)S(1)} %get-tuple-element.58), channel_id=1, source_target_pairs={{0,24},{4,28},{8,16},{12,20},{16,8},{20,12},{24,0},{28,4},{1,25},{... | collective-permute-start | bytes 368648 | tf_op jit(solution)/shard_map/ppermute | solution.py:144
  102.1 1.5 collective-permute-start.37
  104.8 1.4 collective-permute-start.23
  106.3 6.0 %collective-permute-done.12 = bf16[96,640]{1,0:T(8,128)(2,1)S(1)} collective-permute-done((bf16[96,640]{1,0:T(8,128)(2,1)S(1)}, bf16[96,640]{1,0:T(8,128)(2,1)S(1)}, u32[]{:S(2)}, u32[]{:S(2)}) %collective-permute-start.12) | collective-permute-done | bytes 122912 | tf_op jit(solution)/shard_map/ppermute | solution.py:144
  113.8 4.3 %collective-permute-start.14 = (bf16[480,128]{1,0:T(8,128)(2,1)S(1)}, bf16[480,128]{1,0:T(8,128)(2,1)S(1)}, u32[]{:S(2)}, u32[]{:S(2)}) collective-permute-start(bf16[480,128]{1,0:T(8,128)(2,1)S(1)} %pad_maximum_fusion.6), channel_id=1, source_target_pairs={{0,8},{4,12},{8,0},{12,4},{16,24},{20,28},{24,16},{28,20},{1,9},{5... | collective-permute-start | bytes 368648 | tf_op jit(solution)/shard_map/ppermute | solution.py:144
  118.2 3.0 %collective-permute-done.37 = bf16[2,320,640]{2,1,0:T(8,128)(2,1)S(1)} collective-permute-done((bf16[2,320,640]{2,1,0:T(8,128)(2,1)S(1)}, bf16[2,320,640]{2,1,0:T(8,128)(2,1)S(1)}, u32[]{:S(2)}, u32[]{:S(2)}) %collective-permute-start.37) | collective-permute-done | bytes 819232 | tf_op jit(solution)/shard_map/ppermute | solution.py:141
  121.2 1.7 collective-permute-start.15
  125.5 1.3 collective-permute-start.16
  127.3 2.6 %collective-permute-start.8 = (bf16[480,128]{1,0:T(8,128)(2,1)}, bf16[480,128]{1,0:T(8,128)(2,1)S(1)}, u32[]{:S(2)}, u32[]{:S(2)}) collective-permute-start(bf16[480,128]{1,0:T(8,128)(2,1)} %pad_maximum_fusion.4), channel_id=1, source_target_pairs={{0,16},{4,20},{8,24},{12,28},{16,0},{20,4},{24,8},{28,12},{1,17},{... | collective-permute-start | bytes 368648 | tf_op jit(solution)/shard_map/ppermute | solution.py:144
  130.7 1.3 collective-permute-start.9
  132.1 3.0 %collective-permute-done.15 = bf16[480,128]{1,0:T(8,128)(2,1)S(1)} collective-permute-done((bf16[480,128]{1,0:T(8,128)(2,1)S(1)}, bf16[480,128]{1,0:T(8,128)(2,1)S(1)}, u32[]{:S(2)}, u32[]{:S(2)}) %collective-permute-start.15) | collective-permute-done | bytes 122912 | tf_op jit(solution)/shard_map/ppermute | solution.py:144
  135.1 5.0 %collective-permute-start.31 = (bf16[96,128]{1,0:T(8,128)(2,1)}, bf16[96,128]{1,0:T(8,128)(2,1)}, u32[]{:S(2)}, u32[]{:S(2)}) collective-permute-start(bf16[96,128]{1,0:T(8,128)(2,1)} %get-tuple-element.6), channel_id=1, source_target_pairs={{0,16},{4,20},{8,24},{12,28},{16,0},{20,4},{24,8},{28,12},{1,17},{... | collective-permute-start | bytes 73736 | tf_op jit(solution)/shard_map/ppermute | solution.py:144
  141.9 3.4 %collective-permute-start.32 = (bf16[96,128]{1,0:T(8,128)(2,1)}, bf16[96,128]{1,0:T(8,128)(2,1)S(1)}, u32[]{:S(2)}, u32[]{:S(2)}) collective-permute-start(bf16[96,128]{1,0:T(8,128)(2,1)} %get-tuple-element.6), channel_id=1, source_target_pairs={{0,24},{4,28},{8,16},{12,20},{16,8},{20,12},{24,0},{28,4},{1,25},{... | collective-permute-start | bytes 73736 | tf_op jit(solution)/shard_map/ppermute | solution.py:144
  145.3 1.3 constant_dynamic-update-slice_fusion.4
  152.2 3.4 %collective-permute-start.28 = (bf16[96,128]{1,0:T(8,128)(2,1)S(1)}, bf16[96,128]{1,0:T(8,128)(2,1)S(1)}, u32[]{:S(2)}, u32[]{:S(2)}) collective-permute-start(bf16[96,128]{1,0:T(8,128)(2,1)S(1)} %get-tuple-element.10), channel_id=1, source_target_pairs={{0,24},{4,28},{8,16},{12,20},{16,8},{20,12},{24,0},{28,4},{1,25},{... | collective-permute-start | bytes 73736 | tf_op jit(solution)/shard_map/ppermute | solution.py:144
  155.7 1.5 collective-permute-start.25
  158.5 1.6 collective-permute-start.33
  163.0 1.7 collective-permute-done.29
  165.6 1.8 collective-permute-start.35
  167.4 2.6 %collective-permute-start.36 = (bf16[480,128]{1,0:T(8,128)(2,1)S(1)}, bf16[480,128]{1,0:T(8,128)(2,1)S(1)}, u32[]{:S(2)}, u32[]{:S(2)}) collective-permute-start(bf16[480,128]{1,0:T(8,128)(2,1)S(1)} %pad_maximum_fusion.12), channel_id=1, source_target_pairs={{0,24},{4,28},{8,16},{12,20},{16,8},{20,12},{24,0},{28,4},{1,25},{... | collective-permute-start | bytes 368648 | tf_op jit(solution)/shard_map/ppermute | solution.py:144
  170.0 1.6 collective-permute-done.34
  171.8 2.4 %collective-permute-done.36 = bf16[480,128]{1,0:T(8,128)(2,1)S(1)} collective-permute-done((bf16[480,128]{1,0:T(8,128)(2,1)S(1)}, bf16[480,128]{1,0:T(8,128)(2,1)S(1)}, u32[]{:S(2)}, u32[]{:S(2)}) %collective-permute-start.36) | collective-permute-done | bytes 122912 | tf_op jit(solution)/shard_map/ppermute | solution.py:144
  176.0 1.8 collective-permute-done.41
  178.6 7.5 %collective-permute-done.42 = bf16[2,4,24,640]{3,2,1,0:T(8,128)(2,1)S(1)} collective-permute-done((bf16[2,4,24,640]{3,2,1,0:T(8,128)(2,1)S(1)}, bf16[2,4,24,640]{3,2,1,0:T(8,128)(2,1)S(1)}, u32[]{:S(2)}, u32[]{:S(2)}) %collective-permute-start.42) | collective-permute-done | bytes 245792 | tf_op jit(solution)/shard_map/ppermute | solution.py:147
  186.2 1.8 collective-permute-start.43
  187.9 1.4 collective-permute-start.44
  189.3 1.3 collective-permute-start.45
  190.7 3.5 %collective-permute-done.44 = bf16[2,24,640]{2,1,0:T(8,128)(2,1)S(1)} collective-permute-done((bf16[2,24,640]{2,1,0:T(8,128)(2,1)S(1)}, bf16[2,24,640]{2,1,0:T(8,128)(2,1)S(1)}, u32[]{:S(2)}, u32[]{:S(2)}) %collective-permute-start.44) | collective-permute-done | bytes 61472 | tf_op jit(solution)/shard_map/ppermute | solution.py:144
  195.5 2.3 %dynamic_update_slice.15 = bf16[2,24,4,640]{3,2,1,0:T(4,128)(2,1)S(1)} dynamic-update-slice(bf16[2,24,4,640]{3,2,1,0:T(4,128)(2,1)S(1)} %copy.15, bf16[2,24,1,640]{3,2,1,0:T(2,128)(2,1)S(1)} %copy.16, s32[]{:T(128)} %constant.87.clone.1, s32[]{:T(128)} %constant.87.clone.1, s32[]{:T(128)S(6)} %select_n.142, s32[]{:T(128)} %constant.87.clone.1) | dynamic-update-slice | bytes 122884 | tf_op jit(solution)/shard_map/dynamic_update_slice | solution.py:269
  197.9 1.7 add_convert_fusion.1
  (203 shorter events, 36.6 us)
Async XLA Ops:
  2.0 62.0 %collective-permute-start.19 = (bf16[96,640]{1,0:T(8,128)(2,1)}, bf16[96,640]{1,0:T(8,128)(2,1)}, u32[]{:S(2)}, u32[]{:S(2)}) collective-permute-start(bf16[96,640]{1,0:T(8,128)(2,1)} %get-tuple-element.57), channel_id=1, source_target_pairs={{0,8},{4,12},{8,0},{12,4},{16,24},{20,28},{24,16},{28,20},{1,9},{5... | collective-permute-start | bytes 368648 | tf_op jit(solution)/shard_map/ppermute | solution.py:144
  5.1 63.3 %collective-permute-start.20 = (bf16[96,640]{1,0:T(8,128)(2,1)}, bf16[96,640]{1,0:T(8,128)(2,1)}, u32[]{:S(2)}, u32[]{:S(2)}) collective-permute-start(bf16[96,640]{1,0:T(8,128)(2,1)} %get-tuple-element.57), channel_id=1, source_target_pairs={{0,16},{4,20},{8,24},{12,28},{16,0},{20,4},{24,8},{28,12},{1,17},{... | collective-permute-start | bytes 368648 | tf_op jit(solution)/shard_map/ppermute | solution.py:144
  9.2 15.3 %collective-permute-start = (bf16[2,24,640]{2,1,0:T(8,128)(2,1)}, bf16[2,24,640]{2,1,0:T(8,128)(2,1)}, u32[]{:S(2)}, u32[]{:S(2)}) collective-permute-start(bf16[2,24,640]{2,1,0:T(8,128)(2,1)} %pad_maximum_fusion.19), channel_id=1, source_target_pairs={{0,8},{4,12},{8,0},{12,4},{16,24},{20,28},{24,16},{28,20},{1,9},{5... | collective-permute-start | bytes 184328 | tf_op jit(solution)/shard_map/ppermute | solution.py:144
  10.3 14.1 %collective-permute-start.1 = (bf16[2,24,640]{2,1,0:T(8,128)(2,1)}, bf16[2,24,640]{2,1,0:T(8,128)(2,1)}, u32[]{:S(2)}, u32[]{:S(2)}) collective-permute-start(bf16[2,24,640]{2,1,0:T(8,128)(2,1)} %pad_maximum_fusion.20), channel_id=1, source_target_pairs={{0,16},{4,20},{8,24},{12,28},{16,0},{20,4},{24,8},{28,12},{1,17},{... | collective-permute-start | bytes 184328 | tf_op jit(solution)/shard_map/ppermute | solution.py:144
  11.1 13.9 %collective-permute-start.2 = (bf16[2,24,640]{2,1,0:T(8,128)(2,1)}, bf16[2,24,640]{2,1,0:T(8,128)(2,1)}, u32[]{:S(2)}, u32[]{:S(2)}) collective-permute-start(bf16[2,24,640]{2,1,0:T(8,128)(2,1)} %pad_maximum_fusion.21), channel_id=1, source_target_pairs={{0,24},{4,28},{8,16},{12,20},{16,8},{20,12},{24,0},{28,4},{1,25},{... | collective-permute-start | bytes 184328 | tf_op jit(solution)/shard_map/ppermute | solution.py:144
  24.5 17.7 %collective-permute-start.38 = (bf16[96,640]{1,0:T(8,128)(2,1)}, bf16[96,640]{1,0:T(8,128)(2,1)S(1)}, u32[]{:S(2)}, u32[]{:S(2)}) collective-permute-start(bf16[96,640]{1,0:T(8,128)(2,1)} %add_convert_fusion.2), channel_id=1, source_target_pairs={{0,8},{4,12},{8,0},{12,4},{16,24},{20,28},{24,16},{28,20},{1,9},{5... | collective-permute-start | bytes 368648 | tf_op jit(solution)/shard_map/ppermute | solution.py:144
  24.5 18.0 %collective-permute-start.39 = (bf16[96,640]{1,0:T(8,128)(2,1)}, bf16[96,640]{1,0:T(8,128)(2,1)S(1)}, u32[]{:S(2)}, u32[]{:S(2)}) collective-permute-start(bf16[96,640]{1,0:T(8,128)(2,1)} %add_convert_fusion.2), channel_id=1, source_target_pairs={{0,16},{4,20},{8,24},{12,28},{16,0},{20,4},{24,8},{28,12},{1,17},{... | collective-permute-start | bytes 368648 | tf_op jit(solution)/shard_map/ppermute | solution.py:144
  25.1 18.9 %collective-permute-start.40 = (bf16[96,640]{1,0:T(8,128)(2,1)}, bf16[96,640]{1,0:T(8,128)(2,1)S(1)}, u32[]{:S(2)}, u32[]{:S(2)}) collective-permute-start(bf16[96,640]{1,0:T(8,128)(2,1)} %add_convert_fusion.2), channel_id=1, source_target_pairs={{0,24},{4,28},{8,16},{12,20},{16,8},{20,12},{24,0},{28,4},{1,25},{... | collective-permute-start | bytes 368648 | tf_op jit(solution)/shard_map/ppermute | solution.py:144
  42.2 26.3 %collective-permute-start.21 = (bf16[96,640]{1,0:T(8,128)(2,1)}, bf16[96,640]{1,0:T(8,128)(2,1)S(1)}, u32[]{:S(2)}, u32[]{:S(2)}) collective-permute-start(bf16[96,640]{1,0:T(8,128)(2,1)} %get-tuple-element.57), channel_id=1, source_target_pairs={{0,24},{4,28},{8,16},{12,20},{16,8},{20,12},{24,0},{28,4},{1,25},{... | collective-permute-start | bytes 368648 | tf_op jit(solution)/shard_map/ppermute | solution.py:144
  42.5 21.1 %collective-permute-start.18 = (bf16[2,320,640]{2,1,0:T(8,128)(2,1)S(1)}, bf16[2,320,640]{2,1,0:T(8,128)(2,1)S(1)}, u32[]{:S(2)}, u32[]{:S(2)}) collective-permute-start(bf16[2,320,640]{2,1,0:T(8,128)(2,1)S(1)} %copy-done.3), channel_id=1, source_target_pairs={{0,4},{4,0},{8,12},{12,8},{16,20},{20,16},{24,28},{28,24},{1,5},{5... | collective-permute-start | bytes 2457608 | tf_op jit(solution)/shard_map/ppermute | solution.py:141
  44.0 37.1 %collective-permute-start.3 = (bf16[2,320,640]{2,1,0:T(8,128)(2,1)S(1)}, bf16[2,320,640]{2,1,0:T(8,128)(2,1)S(1)}, u32[]{:S(2)}, u32[]{:S(2)}) collective-permute-start(bf16[2,320,640]{2,1,0:T(8,128)(2,1)S(1)} %copy-done.2), channel_id=1, source_target_pairs={{0,4},{4,0},{8,12},{12,8},{16,20},{20,16},{24,28},{28,24},{1,5},{5... | collective-permute-start | bytes 2457608 | tf_op jit(solution)/shard_map/ppermute | solution.py:141
  44.8 23.7 %copy-start.13 = (bf16[4,2,2,24,640]{4,3,2,1,0:T(8,128)(2,1)}, bf16[4,2,2,24,640]{4,3,2,1,0:T(8,128)(2,1)S(1)}, u32[]{:S(2)}) copy-start(bf16[4,2,2,24,640]{4,3,2,1,0:T(8,128)(2,1)S(1)} %constant_dynamic-update-slice_fusion.20) | copy-start | bytes 1474564
  63.5 35.3 %collective-permute-start.4 = (bf16[96,640]{1,0:T(8,128)(2,1)S(1)}, bf16[96,640]{1,0:T(8,128)(2,1)S(1)}, u32[]{:S(2)}, u32[]{:S(2)}) collective-permute-start(bf16[96,640]{1,0:T(8,128)(2,1)S(1)} %get-tuple-element.59), channel_id=1, source_target_pairs={{0,8},{4,12},{8,0},{12,4},{16,24},{20,28},{24,16},{28,20},{1,9},{5... | collective-permute-start | bytes 368648 | tf_op jit(solution)/shard_map/ppermute | solution.py:144
  64.1 38.0 %collective-permute-start.5 = (bf16[96,640]{1,0:T(8,128)(2,1)S(1)}, bf16[96,640]{1,0:T(8,128)(2,1)S(1)}, u32[]{:S(2)}, u32[]{:S(2)}) collective-permute-start(bf16[96,640]{1,0:T(8,128)(2,1)S(1)} %get-tuple-element.59), channel_id=1, source_target_pairs={{0,16},{4,20},{8,24},{12,28},{16,0},{20,4},{24,8},{28,12},{1,17},{... | collective-permute-start | bytes 368648 | tf_op jit(solution)/shard_map/ppermute | solution.py:144
  68.3 35.3 %collective-permute-start.6 = (bf16[96,640]{1,0:T(8,128)(2,1)S(1)}, bf16[96,640]{1,0:T(8,128)(2,1)S(1)}, u32[]{:S(2)}, u32[]{:S(2)}) collective-permute-start(bf16[96,640]{1,0:T(8,128)(2,1)S(1)} %get-tuple-element.59), channel_id=1, source_target_pairs={{0,24},{4,28},{8,16},{12,20},{16,8},{20,12},{24,0},{28,4},{1,25},{... | collective-permute-start | bytes 368648 | tf_op jit(solution)/shard_map/ppermute | solution.py:144
  68.5 29.5 %collective-permute-start.10 = (bf16[2,320,640]{2,1,0:T(8,128)(2,1)S(1)}, bf16[2,320,640]{2,1,0:T(8,128)(2,1)S(1)}, u32[]{:S(2)}, u32[]{:S(2)}) collective-permute-start(bf16[2,320,640]{2,1,0:T(8,128)(2,1)S(1)} %get-tuple-element.18), channel_id=1, source_target_pairs={{0,4},{4,0},{8,12},{12,8},{16,20},{20,16},{24,28},{28,24},{1,5},{5... | collective-permute-start | bytes 2457608 | tf_op jit(solution)/shard_map/ppermute | solution.py:141
  81.1 23.7 %collective-permute-start.11 = (bf16[96,640]{1,0:T(8,128)(2,1)S(1)}, bf16[96,640]{1,0:T(8,128)(2,1)S(1)}, u32[]{:S(2)}, u32[]{:S(2)}) collective-permute-start(bf16[96,640]{1,0:T(8,128)(2,1)S(1)} %get-tuple-element.58), channel_id=1, source_target_pairs={{0,8},{4,12},{8,0},{12,4},{16,24},{20,28},{24,16},{28,20},{1,9},{5... | collective-permute-start | bytes 368648 | tf_op jit(solution)/shard_map/ppermute | solution.py:144
  81.6 20.5 %copy-start.4 = (bf16[2,640,320]{1,2,0:T(8,128)(2,1)S(1)}, bf16[2,640,320]{1,2,0:T(8,128)(2,1)}, u32[]{:S(2)}) copy-start(bf16[2,640,320]{1,2,0:T(8,128)(2,1)} %param.15) | copy-start | bytes 2457604
  98.0 14.2 %collective-permute-start.12 = (bf16[96,640]{1,0:T(8,128)(2,1)S(1)}, bf16[96,640]{1,0:T(8,128)(2,1)S(1)}, u32[]{:S(2)}, u32[]{:S(2)}) collective-permute-start(bf16[96,640]{1,0:T(8,128)(2,1)S(1)} %get-tuple-element.58), channel_id=1, source_target_pairs={{0,16},{4,20},{8,24},{12,28},{16,0},{20,4},{24,8},{28,12},{1,17},{... | collective-permute-start | bytes 368648 | tf_op jit(solution)/shard_map/ppermute | solution.py:144
  98.8 13.7 %collective-permute-start.13 = (bf16[96,640]{1,0:T(8,128)(2,1)S(1)}, bf16[96,640]{1,0:T(8,128)(2,1)S(1)}, u32[]{:S(2)}, u32[]{:S(2)}) collective-permute-start(bf16[96,640]{1,0:T(8,128)(2,1)S(1)} %get-tuple-element.58), channel_id=1, source_target_pairs={{0,24},{4,28},{8,16},{12,20},{16,8},{20,12},{24,0},{28,4},{1,25},{... | collective-permute-start | bytes 368648 | tf_op jit(solution)/shard_map/ppermute | solution.py:144
  102.1 19.1 %collective-permute-start.37 = (bf16[2,320,640]{2,1,0:T(8,128)(2,1)S(1)}, bf16[2,320,640]{2,1,0:T(8,128)(2,1)S(1)}, u32[]{:S(2)}, u32[]{:S(2)}) collective-permute-start(bf16[2,320,640]{2,1,0:T(8,128)(2,1)S(1)} %bitcast.290), channel_id=1, source_target_pairs={{0,4},{4,0},{8,12},{12,8},{16,20},{20,16},{24,28},{28,24},{1,5},{5... | collective-permute-start | bytes 2457608 | tf_op jit(solution)/shard_map/ppermute | solution.py:141
  103.6 21.8 %collective-permute-start.22 = (bf16[480,128]{1,0:T(8,128)(2,1)S(1)}, bf16[480,128]{1,0:T(8,128)(2,1)S(1)}, u32[]{:S(2)}, u32[]{:S(2)}) collective-permute-start(bf16[480,128]{1,0:T(8,128)(2,1)S(1)} %pad_maximum_fusion.9), channel_id=1, source_target_pairs={{0,8},{4,12},{8,0},{12,4},{16,24},{20,28},{24,16},{28,20},{1,9},{5... | collective-permute-start | bytes 368648 | tf_op jit(solution)/shard_map/ppermute | solution.py:144
  104.8 22.0 %collective-permute-start.23 = (bf16[480,128]{1,0:T(8,128)(2,1)S(1)}, bf16[480,128]{1,0:T(8,128)(2,1)S(1)}, u32[]{:S(2)}, u32[]{:S(2)}) collective-permute-start(bf16[480,128]{1,0:T(8,128)(2,1)S(1)} %pad_maximum_fusion.10), channel_id=1, source_target_pairs={{0,16},{4,20},{8,24},{12,28},{16,0},{20,4},{24,8},{28,12},{1,17},{... | collective-permute-start | bytes 368648 | tf_op jit(solution)/shard_map/ppermute | solution.py:144
  112.2 15.0 %collective-permute-start.24 = (bf16[480,128]{1,0:T(8,128)(2,1)S(1)}, bf16[480,128]{1,0:T(8,128)(2,1)S(1)}, u32[]{:S(2)}, u32[]{:S(2)}) collective-permute-start(bf16[480,128]{1,0:T(8,128)(2,1)S(1)} %pad_maximum_fusion.11), channel_id=1, source_target_pairs={{0,24},{4,28},{8,16},{12,20},{16,8},{20,12},{24,0},{28,4},{1,25},{... | collective-permute-start | bytes 368648 | tf_op jit(solution)/shard_map/ppermute | solution.py:144
  113.8 16.9 %collective-permute-start.14 = (bf16[480,128]{1,0:T(8,128)(2,1)S(1)}, bf16[480,128]{1,0:T(8,128)(2,1)S(1)}, u32[]{:S(2)}, u32[]{:S(2)}) collective-permute-start(bf16[480,128]{1,0:T(8,128)(2,1)S(1)} %pad_maximum_fusion.6), channel_id=1, source_target_pairs={{0,8},{4,12},{8,0},{12,4},{16,24},{20,28},{24,16},{28,20},{1,9},{5... | collective-permute-start | bytes 368648 | tf_op jit(solution)/shard_map/ppermute | solution.py:144
  121.2 13.9 %collective-permute-start.15 = (bf16[480,128]{1,0:T(8,128)(2,1)S(1)}, bf16[480,128]{1,0:T(8,128)(2,1)S(1)}, u32[]{:S(2)}, u32[]{:S(2)}) collective-permute-start(bf16[480,128]{1,0:T(8,128)(2,1)S(1)} %pad_maximum_fusion.7), channel_id=1, source_target_pairs={{0,16},{4,20},{8,24},{12,28},{16,0},{20,4},{24,8},{28,12},{1,17},{... | collective-permute-start | bytes 368648 | tf_op jit(solution)/shard_map/ppermute | solution.py:144
  125.5 9.6 %collective-permute-start.16 = (bf16[480,128]{1,0:T(8,128)(2,1)S(1)}, bf16[480,128]{1,0:T(8,128)(2,1)S(1)}, u32[]{:S(2)}, u32[]{:S(2)}) collective-permute-start(bf16[480,128]{1,0:T(8,128)(2,1)S(1)} %pad_maximum_fusion.8), channel_id=1, source_target_pairs={{0,24},{4,28},{8,16},{12,20},{16,8},{20,12},{24,0},{28,4},{1,25},{... | collective-permute-start | bytes 368648 | tf_op jit(solution)/shard_map/ppermute | solution.py:144
  126.8 15.1 %collective-permute-start.7 = (bf16[480,128]{1,0:T(8,128)(2,1)}, bf16[480,128]{1,0:T(8,128)(2,1)S(1)}, u32[]{:S(2)}, u32[]{:S(2)}) collective-permute-start(bf16[480,128]{1,0:T(8,128)(2,1)} %pad_maximum_fusion.3), channel_id=1, source_target_pairs={{0,8},{4,12},{8,0},{12,4},{16,24},{20,28},{24,16},{28,20},{1,9},{5... | collective-permute-start | bytes 368648 | tf_op jit(solution)/shard_map/ppermute | solution.py:144
  127.3 19.3 %collective-permute-start.8 = (bf16[480,128]{1,0:T(8,128)(2,1)}, bf16[480,128]{1,0:T(8,128)(2,1)S(1)}, u32[]{:S(2)}, u32[]{:S(2)}) collective-permute-start(bf16[480,128]{1,0:T(8,128)(2,1)} %pad_maximum_fusion.4), channel_id=1, source_target_pairs={{0,16},{4,20},{8,24},{12,28},{16,0},{20,4},{24,8},{28,12},{1,17},{... | collective-permute-start | bytes 368648 | tf_op jit(solution)/shard_map/ppermute | solution.py:144
  130.7 15.9 %collective-permute-start.9 = (bf16[480,128]{1,0:T(8,128)(2,1)}, bf16[480,128]{1,0:T(8,128)(2,1)S(1)}, u32[]{:S(2)}, u32[]{:S(2)}) collective-permute-start(bf16[480,128]{1,0:T(8,128)(2,1)} %pad_maximum_fusion.5), channel_id=1, source_target_pairs={{0,24},{4,28},{8,16},{12,20},{16,8},{20,12},{24,0},{28,4},{1,25},{... | collective-permute-start | bytes 368648 | tf_op jit(solution)/shard_map/ppermute | solution.py:144
  135.1 17.1 %collective-permute-start.30 = (bf16[96,128]{1,0:T(8,128)(2,1)}, bf16[96,128]{1,0:T(8,128)(2,1)}, u32[]{:S(2)}, u32[]{:S(2)}) collective-permute-start(bf16[96,128]{1,0:T(8,128)(2,1)} %get-tuple-element.6), channel_id=1, source_target_pairs={{0,8},{4,12},{8,0},{12,4},{16,24},{20,28},{24,16},{28,20},{1,9},{5... | collective-permute-start | bytes 73736 | tf_op jit(solution)/shard_map/ppermute | solution.py:144
  135.1 20.6 %collective-permute-start.31 = (bf16[96,128]{1,0:T(8,128)(2,1)}, bf16[96,128]{1,0:T(8,128)(2,1)}, u32[]{:S(2)}, u32[]{:S(2)}) collective-permute-start(bf16[96,128]{1,0:T(8,128)(2,1)} %get-tuple-element.6), channel_id=1, source_target_pairs={{0,16},{4,20},{8,24},{12,28},{16,0},{20,4},{24,8},{28,12},{1,17},{... | collective-permute-start | bytes 73736 | tf_op jit(solution)/shard_map/ppermute | solution.py:144
  141.9 15.3 %collective-permute-start.32 = (bf16[96,128]{1,0:T(8,128)(2,1)}, bf16[96,128]{1,0:T(8,128)(2,1)S(1)}, u32[]{:S(2)}, u32[]{:S(2)}) collective-permute-start(bf16[96,128]{1,0:T(8,128)(2,1)} %get-tuple-element.6), channel_id=1, source_target_pairs={{0,24},{4,28},{8,16},{12,20},{16,8},{20,12},{24,0},{28,4},{1,25},{... | collective-permute-start | bytes 73736 | tf_op jit(solution)/shard_map/ppermute | solution.py:144
  146.6 11.9 %collective-permute-start.26 = (bf16[96,128]{1,0:T(8,128)(2,1)S(1)}, bf16[96,128]{1,0:T(8,128)(2,1)S(1)}, u32[]{:S(2)}, u32[]{:S(2)}) collective-permute-start(bf16[96,128]{1,0:T(8,128)(2,1)S(1)} %get-tuple-element.10), channel_id=1, source_target_pairs={{0,8},{4,12},{8,0},{12,4},{16,24},{20,28},{24,16},{28,20},{1,9},{5... | collective-permute-start | bytes 73736 | tf_op jit(solution)/shard_map/ppermute | solution.py:144
  146.7 13.4 %collective-permute-start.27 = (bf16[96,128]{1,0:T(8,128)(2,1)S(1)}, bf16[96,128]{1,0:T(8,128)(2,1)S(1)}, u32[]{:S(2)}, u32[]{:S(2)}) collective-permute-start(bf16[96,128]{1,0:T(8,128)(2,1)S(1)} %get-tuple-element.10), channel_id=1, source_target_pairs={{0,16},{4,20},{8,24},{12,28},{16,0},{20,4},{24,8},{28,12},{1,17},{... | collective-permute-start | bytes 73736 | tf_op jit(solution)/shard_map/ppermute | solution.py:144
  152.2 7.8 %collective-permute-start.28 = (bf16[96,128]{1,0:T(8,128)(2,1)S(1)}, bf16[96,128]{1,0:T(8,128)(2,1)S(1)}, u32[]{:S(2)}, u32[]{:S(2)}) collective-permute-start(bf16[96,128]{1,0:T(8,128)(2,1)S(1)} %get-tuple-element.10), channel_id=1, source_target_pairs={{0,24},{4,28},{8,16},{12,20},{16,8},{20,12},{24,0},{28,4},{1,25},{... | collective-permute-start | bytes 73736 | tf_op jit(solution)/shard_map/ppermute | solution.py:144
  155.7 7.0 %collective-permute-start.25 = (bf16[384,128]{1,0:T(8,128)(2,1)S(1)}, bf16[384,128]{1,0:T(8,128)(2,1)S(1)}, u32[]{:S(2)}, u32[]{:S(2)}) collective-permute-start(bf16[384,128]{1,0:T(8,128)(2,1)S(1)} %bitcast.301), channel_id=1, source_target_pairs={{0,4},{4,0},{8,12},{12,8},{16,20},{20,16},{24,28},{28,24},{1,5},{5... | collective-permute-start | bytes 294920 | tf_op jit(solution)/shard_map/ppermute | solution.py:141
  157.2 5.1 %collective-permute-start.17 = (bf16[384,128]{1,0:T(8,128)(2,1)S(1)}, bf16[384,128]{1,0:T(8,128)(2,1)S(1)}, u32[]{:S(2)}, u32[]{:S(2)}) collective-permute-start(bf16[384,128]{1,0:T(8,128)(2,1)S(1)} %fusion.56), channel_id=1, source_target_pairs={{0,4},{4,0},{8,12},{12,8},{16,20},{20,16},{24,28},{28,24},{1,5},{5... | collective-permute-start | bytes 294920 | tf_op jit(solution)/shard_map/ppermute | solution.py:141
  158.5 6.6 %collective-permute-start.33 = (bf16[384,128]{1,0:T(8,128)(2,1)S(1)}, bf16[384,128]{1,0:T(8,128)(2,1)S(1)}, u32[]{:S(2)}, u32[]{:S(2)}) collective-permute-start(bf16[384,128]{1,0:T(8,128)(2,1)S(1)} %pad_maximum_fusion.14), channel_id=1, source_target_pairs={{0,4},{4,0},{8,12},{12,8},{16,20},{20,16},{24,28},{28,24},{1,5},{5... | collective-permute-start | bytes 294920 | tf_op jit(solution)/shard_map/ppermute | solution.py:141
  160.1 4.7 %collective-permute-start.29 = (bf16[384,128]{1,0:T(8,128)(2,1)S(1)}, bf16[384,128]{1,0:T(8,128)(2,1)S(1)}, u32[]{:S(2)}, u32[]{:S(2)}) collective-permute-start(bf16[384,128]{1,0:T(8,128)(2,1)S(1)} %pad_maximum_fusion.13), channel_id=1, source_target_pairs={{0,4},{4,0},{8,12},{12,8},{16,20},{20,16},{24,28},{28,24},{1,5},{5... | collective-permute-start | bytes 294920 | tf_op jit(solution)/shard_map/ppermute | solution.py:141
  165.4 6.3 %collective-permute-start.34 = (bf16[480,128]{1,0:T(8,128)(2,1)S(1)}, bf16[480,128]{1,0:T(8,128)(2,1)S(1)}, u32[]{:S(2)}, u32[]{:S(2)}) collective-permute-start(bf16[480,128]{1,0:T(8,128)(2,1)S(1)} %pad_maximum_fusion.12), channel_id=1, source_target_pairs={{0,8},{4,12},{8,0},{12,4},{16,24},{20,28},{24,16},{28,20},{1,9},{5... | collective-permute-start | bytes 368648 | tf_op jit(solution)/shard_map/ppermute | solution.py:144
  165.6 6.1 %collective-permute-start.35 = (bf16[480,128]{1,0:T(8,128)(2,1)S(1)}, bf16[480,128]{1,0:T(8,128)(2,1)S(1)}, u32[]{:S(2)}, u32[]{:S(2)}) collective-permute-start(bf16[480,128]{1,0:T(8,128)(2,1)S(1)} %pad_maximum_fusion.12), channel_id=1, source_target_pairs={{0,16},{4,20},{8,24},{12,28},{16,0},{20,4},{24,8},{28,12},{1,17},{... | collective-permute-start | bytes 368648 | tf_op jit(solution)/shard_map/ppermute | solution.py:144
  167.4 6.9 %collective-permute-start.36 = (bf16[480,128]{1,0:T(8,128)(2,1)S(1)}, bf16[480,128]{1,0:T(8,128)(2,1)S(1)}, u32[]{:S(2)}, u32[]{:S(2)}) collective-permute-start(bf16[480,128]{1,0:T(8,128)(2,1)S(1)} %pad_maximum_fusion.12), channel_id=1, source_target_pairs={{0,24},{4,28},{8,16},{12,20},{16,8},{20,12},{24,0},{28,4},{1,25},{... | collective-permute-start | bytes 368648 | tf_op jit(solution)/shard_map/ppermute | solution.py:144
  175.9 1.9 collective-permute-start.41
  178.0 8.1 %collective-permute-start.42 = (bf16[2,4,24,640]{3,2,1,0:T(8,128)(2,1)S(1)}, bf16[2,4,24,640]{3,2,1,0:T(8,128)(2,1)S(1)}, u32[]{:S(2)}, u32[]{:S(2)}) collective-permute-start(bf16[2,4,24,640]{3,2,1,0:T(8,128)(2,1)S(1)} %fusion.48), channel_id=1, source_target_pairs={{0,2},{1,3},{2,0},{3,1},{4,6},{5,7},{6,4},{7,5},{8,10},{9,11},{10,... | collective-permute-start | bytes 737288 | tf_op jit(solution)/shard_map/ppermute | solution.py:147
  186.2 4.5 %collective-permute-start.43 = (bf16[2,24,640]{2,1,0:T(8,128)(2,1)S(1)}, bf16[2,24,640]{2,1,0:T(8,128)(2,1)S(1)}, u32[]{:S(2)}, u32[]{:S(2)}) collective-permute-start(bf16[2,24,640]{2,1,0:T(8,128)(2,1)S(1)} %get-tuple-element.64), channel_id=1, source_target_pairs={{0,8},{4,12},{8,0},{12,4},{16,24},{20,28},{24,16},{28,20},{1,9},{5... | collective-permute-start | bytes 184328 | tf_op jit(solution)/shard_map/ppermute | solution.py:144
  187.9 6.3 %collective-permute-start.44 = (bf16[2,24,640]{2,1,0:T(8,128)(2,1)S(1)}, bf16[2,24,640]{2,1,0:T(8,128)(2,1)S(1)}, u32[]{:S(2)}, u32[]{:S(2)}) collective-permute-start(bf16[2,24,640]{2,1,0:T(8,128)(2,1)S(1)} %get-tuple-element.63), channel_id=1, source_target_pairs={{0,16},{4,20},{8,24},{12,28},{16,0},{20,4},{24,8},{28,12},{1,17},{... | collective-permute-start | bytes 184328 | tf_op jit(solution)/shard_map/ppermute | solution.py:144
  189.3 6.1 %collective-permute-start.45 = (bf16[2,24,640]{2,1,0:T(8,128)(2,1)S(1)}, bf16[2,24,640]{2,1,0:T(8,128)(2,1)S(1)}, u32[]{:S(2)}, u32[]{:S(2)}) collective-permute-start(bf16[2,24,640]{2,1,0:T(8,128)(2,1)S(1)} %get-tuple-element.62), channel_id=1, source_target_pairs={{0,24},{4,28},{8,16},{12,20},{16,8},{20,12},{24,0},{28,4},{1,25},{... | collective-permute-start | bytes 184328 | tf_op jit(solution)/shard_map/ppermute | solution.py:144
  (16 other events, 107.2 us)

commit v2 on v0

--- a/solution.py
+++ b/solution.py
@@ -1,8 +1,11 @@
+import functools
 import math
 
 import jax
 import jax.numpy as jnp
 from jax import lax
+from jax.experimental import pallas as pl
+from jax.experimental.pallas import tpu as pltpu
 from jax.sharding import PartitionSpec as P
 
 HEAD = 128
@@ -22,7 +25,7 @@
     return (by_head * inverse_rms * gain_vector.reshape(-1, HEAD)).astype(jnp.bfloat16)
 
 
-def body(
+def gather_plan(
     tokens, in_bits, qkv_weights, qkv_bits, gain_query, gain_key, out_weights, mix_bits, out_bits
 ):
     flipped = (tokens.astype(jnp.float32) * signed(in_bits)).astype(jnp.bfloat16)
@@ -94,6 +97,358 @@
     own_signs = lax.dynamic_slice_in_dim(out_signs, lax.axis_index("uly") * own_rows, own_rows, 0)
     result_rows = summed[:, 0] + own_signs * summed[:, 1]
     return result_rows.astype(jnp.bfloat16)
+
+
+def dot32(a, b):
+    return lax.dot_general(
+        a, b, (((1,), (0,)), ((), ())), preferred_element_type=jnp.float32
+    )
+
+
+def dot32_t(a, b):
+    return lax.dot_general(
+        a, b, (((1,), (1,)), ((), ())), preferred_element_type=jnp.float32
+    )
+
+
+bf = jnp.bfloat16
+VMEM = pl.BlockSpec(memory_space=pltpu.VMEM)
+SMEM = pl.BlockSpec(memory_space=pltpu.SMEM)
+ANY = pl.BlockSpec(memory_space=pl.ANY)
+
+
+def call(kernel, outs, out_specs, in_specs, scratch=(), flops=0, moved=0):
+    return pl.pallas_call(
+        kernel,
+        out_shape=outs,
+        in_specs=in_specs,
+        out_specs=out_specs,
+        scratch_shapes=list(scratch),
+        compiler_params=pltpu.CompilerParams(vmem_limit_bytes=40 * 1024 * 1024),
+        cost_estimate=pl.CostEstimate(flops=flops, bytes_accessed=moved, transcendentals=0),
+    )
+
+
+def shape(*dims, dtype=bf):
+    return jax.ShapeDtypeStruct(dims, dtype)
+
+
+def lanes(index, size):
+    return pl.ds(pl.multiple_of(index * size, 128), size)
+
+
+def prepare_kernel(place, tokens, in_bits, sign_bits, weights, value_weights, signs, *blocks):
+    copies = [
+        pltpu.make_async_copy(weights.at[m, 2], value_weights.at[m], blocks[-1].at[m])
+        for m in (0, 1)
+    ]
+    for copy in copies:
+        copy.start()
+    z = place[0]
+    depth = len(blocks) - 1
+    wide = tokens.shape[1] // depth
+    for k in range(depth):
+        cut = lanes(z ^ k, wide)
+        plain = tokens[:, cut]
+        sign = (2 * in_bits[:, cut] - 1).astype(jnp.float32)
+        blocks[k][0] = plain
+        blocks[k][1] = (plain.astype(jnp.float32) * sign).astype(bf)
+    signs[...] = (2 * sign_bits[2] - 1).astype(jnp.float32).astype(bf)
+    for copy in copies:
+        copy.wait()
+
+
+def rest_kernel(sign_bits, mix_bits, weights, key_weights, query_a, query_b, signs, mix, sems):
+    pieces = ((1, 0, key_weights.at[0]), (1, 1, key_weights.at[1]), (0, 0, query_a), (0, 1, query_b))
+    copies = [
+        pltpu.make_async_copy(weights.at[m, part], out, sems.at[part, m])
+        for part, m, out in pieces
+    ]
+    for copy in copies:
+        copy.start()
+    for part in (0, 1):
+        signs[part] = (2 * sign_bits[part] - 1).astype(jnp.float32).astype(bf)
+    mix[...] = (2 * mix_bits[...] - 1).astype(jnp.float32).astype(bf)
+    for copy in copies:
+        copy.wait()
+
+
+def project_kernel(
+    part, whole, place, rows, weights, partner_0, partner_1, sign_0, sign_2, sign_13,
+    send, keep_own, keep_two, held, total, sems,
+):
+    z, x = place[0], place[1]
+    slab, columns = weights.shape[2], weights.shape[3]
+    partner = (partner_0, partner_1)
+    if len(partner_0.shape) == 3:
+        partner = (partner_0.at[0], partner_0.at[1])
+    own = pl.ds(pl.multiple_of(x * slab, 64), slab)
+    other = pl.ds(pl.multiple_of((1 - x) * slab, 64), slab)
+    copies = []
+    for m in (0, 1):
+        copies.append(
+            pltpu.make_async_copy(weights.at[m, part], held.at[m, own], sems.at[m, 0])
+        )
+        copies.append(pltpu.make_async_copy(partner[m], held.at[m, other], sems.at[m, 1]))
+    for copy in copies:
+        copy.start()
+    for copy in copies:
+        copy.wait()
+    size = sign_0.shape[0]
+    depth = rows.shape[1] // size
+    total[...] = dot32(rows[1], held[1])
+    plain = dot32(rows[0], held[0])
+    for j in range(depth):
+        cut = slice(j * size, (j + 1) * size)
+        sign = (sign_0[...], sign_13[0], sign_2[...], sign_13[1])[j].astype(jnp.float32)
+        total[cut] = plain[cut] + sign * total[cut]
+
+    def block(j, head):
+        return total[j * size : (j + 1) * size, lanes(head, HEAD)]
+
+    def main(target, start, k):
+        for j in range(depth):
+            at = start + (j ^ k) * size
+            target[at : at + size] = block(j, z ^ k).astype(target.dtype)
+
+    def rest(target, start, j):
+        target[start : start + size] = block(j, depth).astype(target.dtype)
+
+    half = depth * size
+    if whole:
+        main(send, 0, 1)
+        main(send, half, 3)
+        for j in range(depth):
+            rest(send, 2 * half + (j ^ 1) * size, j)
+            rest(keep_own, half + j * size, j)
+    else:
+        main(send, 0, 1)
+        rest(send, half, 1)
+        main(send, half + size, 3)
+        rest(send, 2 * half + size, 3)
+        rest(keep_own, half, 0)
+        rest(keep_two, half, 2)
+    main(keep_own, 0, 0)
+    main(keep_two, 0, 2)
+
+
+def middle_kernel(size, keep_own, keep_two, taken, send, total):
+    half = 4 * size
+    if taken.shape[0] == 3 * half:
+        total[:half] = keep_own[:half] + taken[:half].astype(jnp.float32)
+        send[:half] = (keep_two[...] + taken[half : 2 * half].astype(jnp.float32)).astype(bf)
+        for j in range(4):
+            cut = slice(half + j * size, half + (j + 1) * size)
+            got = taken[half + cut.start : half + cut.stop].astype(jnp.float32)
+            value = keep_own[cut] + got
+            total[cut] = value
+            at = half + (j ^ 2) * size
+            send[at : at + size] = value.astype(bf)
+    else:
+        count = half + size
+        total[...] = keep_own[...] + taken[:count].astype(jnp.float32)
+        send[...] = (keep_two[...] + taken[count:].astype(jnp.float32)).astype(bf)
+
+
+def norm_rows(values, gain_row):
+    wide = values.astype(jnp.float32)
+    inverse_rms = lax.rsqrt(jnp.mean(wide * wide, axis=-1, keepdims=True) + epsilon)
+    return (wide * inverse_rms * gain_row).astype(bf)
+
+
+def key_kernel(half, place, total, taken, gain, keys):
+    keep = (total[...] + taken[...].astype(jnp.float32)).astype(bf)
+    heads = gain.shape[0]
+    keys[:half] = norm_rows(keep[:half], gain[pl.ds(place[0], 1), :])
+    keys[half:] = norm_rows(keep[half:], gain[heads - 1 : heads, :])
+
+
+def attend_kernel(half, place, total, taken, gain, keys_a, keys_b, values_a, values_b, out):
+    keep = (total[...] + taken[...].astype(jnp.float32)).astype(bf)
+    heads = gain.shape[0]
+
+    def attend(queries, cut):
+        score_scale = 1.0 / math.sqrt(HEAD)
+        totals, sums = 0.0, 0.0
+        for keys, values in ((keys_a, values_a), (keys_b, values_b)):
+            scores = dot32_t(queries, keys[cut]) * score_scale
+            weights = jnp.exp(scores).astype(bf)
+            totals = totals + jnp.sum(weights.astype(jnp.float32), axis=1, keepdims=True)
+            sums = sums + dot32(weights, values[cut])
+        return (sums / totals).astype(bf)
+
+    first = norm_rows(keep[:half], gain[pl.ds(place[0], 1), :])
+    out[:half] = attend(first, slice(0, half))
+    last = norm_rows(keep[half:], gain[heads - 1 : heads, :])
+    out[half:] = attend(last, slice(half, 2 * half))
+
+
+def stationary_plan(
+    tokens, in_bits, qkv_weights, qkv_bits, gain_query, gain_key, out_weights, mix_bits, out_bits
+):
+    groups = lax.axis_size("blk")
+    team = lax.axis_size("uly")
+    depth = groups // 2
+    z = lax.axis_index("blk") // 2
+    x = lax.axis_index("blk") % 2
+    u = lax.axis_index("uly")
+    own_rows, width = tokens.shape
+    slab = qkv_weights.shape[2]
+    columns = qkv_weights.shape[3]
+    size = own_rows * team
+    heads = columns // HEAD
+    half = depth * size
+    steps = range(depth)
+    place = jnp.stack([z, x]).astype(jnp.int32)
+
+    def swap_x(value):
+        return lax.ppermute(value, "blk", [(i, i ^ 1) for i in range(groups)])
+
+    def swap_z(value, step):
+        return lax.ppermute(value, "blk", [(i, i ^ (2 * step)) for i in range(groups)])
+
+    def swap_u(value, bit):
+        return lax.ppermute(value, "uly", [(i, i ^ bit) for i in range(team)])
+
+    def after(value, *earlier):
+        return lax.optimization_barrier((value,) + earlier)[0]
+
+    def gather_z(value):
+        two = swap_z(value, 2)
+        return value, two, swap_z(jnp.stack([value, two]), 1)
+
+    sign_bits = jnp.transpose(qkv_bits, (1, 0, 2))
+    weights_shape = shape(2, slab, columns)
+    prepared = call(
+        prepare_kernel,
+        [weights_shape, shape(size, columns)] + [shape(2, own_rows, 2 * slab)] * depth,
+        [ANY] + [VMEM] * (depth + 1),
+        [SMEM] + [VMEM] * 3 + [ANY],
+        [pltpu.SemaphoreType.DMA((2,))],
+    )(place, tokens, in_bits, sign_bits, qkv_weights)
+    value_weights, sign_value, blocks = prepared[0], prepared[1], prepared[2:]
+    partner = {2: [swap_x(value_weights)] * 2}
+    held = [blocks[0]] + [swap_z(blocks[k], k) for k in steps if k]
+    signs = {2: gather_z(sign_value)}
+
+    piece_shape = shape(slab, columns)
+    key_weights, query_a, query_b, sign_pair, mix_own = call(
+        rest_kernel,
+        [weights_shape, piece_shape, piece_shape, shape(2, size, columns), shape(size, columns)],
+        [ANY, ANY, ANY, VMEM, VMEM],
+        [VMEM, VMEM, ANY],
+        [pltpu.SemaphoreType.DMA((2, 2))],
+    )(after(sign_bits, value_weights), mix_bits, qkv_weights)
+    rows = lax.all_gather(jnp.stack(held), "uly", axis=0)
+    rows = jnp.transpose(rows, (2, 1, 0, 3, 4)).reshape(2, half, 2 * slab)
+
+    partner[1] = [swap_x(after(key_weights, partner[2][0], rows))] * 2
+    query_a = swap_x(after(query_a, partner[1][0]))
+    query_b = swap_x(after(query_b, query_a))
+    partner[0] = [query_a, query_b]
+    out_t = jnp.transpose(out_weights, (0, 2, 1))
+    out_partner = swap_x(after(out_t, query_b))
+
+    pair_0, pair_2, pair_13 = gather_z(after(sign_pair, signs[2][2]))
+    for part in (0, 1):
+        signs[part] = (pair_0[part], pair_2[part], pair_13[:, part])
+
+    def project(part, whole, rows, beside=()):
+        count = 2 * half if whole else half + size
+        f32 = jnp.float32
+        send, keep_own, keep_two = call(
+            functools.partial(project_kernel, part, whole),
+            [
+                shape(3 * half if whole else 2 * count, HEAD),
+                shape(count, HEAD, dtype=f32),
+                shape(half if whole else count, HEAD, dtype=f32),
+            ],
+            [VMEM] * 3,
+            [SMEM, VMEM, ANY, ANY, ANY, VMEM, VMEM, VMEM],
+            [
+                pltpu.VMEM((2, 2 * slab, columns), bf),
+                pltpu.VMEM((half, columns), f32),
+                pltpu.SemaphoreType.DMA((2, 2)),
+            ],
+        )(place, rows, qkv_weights, *partner[part], *signs[part])
+        taken = after(swap_z(send, 1), *beside)
+        send, total = call(
+            functools.partial(middle_kernel, size),
+            [shape(count, HEAD), shape(count, HEAD, dtype=f32)],
+            [VMEM] * 2,
+            [VMEM] * 3,
+        )(keep_own, keep_two, taken)
+        return total, swap_z(send, 2)
+
+    total, taken = project(2, True, rows)
+    values = (total + taken.astype(jnp.float32)).astype(bf)
+    rows_next = after(rows, values)
+    values_partner = swap_x(values)
+    total, taken = project(1, True, rows_next, (query_a,))
+    rows_next = after(rows, total)
+    taken = after(taken, query_b)
+    keys = call(
+        functools.partial(key_kernel, half), shape(2 * half, HEAD), VMEM, [SMEM] + [VMEM] * 3
+    )(place, total, taken, gain_key.reshape(heads, HEAD))
+    keys_partner = swap_x(keys)
+    mix_0, mix_2, mix_13 = gather_z(after(mix_own, keys))
+    total, taken = project(0, False, rows_next)
+    done = call(
+        functools.partial(attend_kernel, half),
+        shape(half + size, HEAD),
+        VMEM,
+        [SMEM] + [VMEM] * 7,
+    )(
+        place, total, taken, gain_query.reshape(heads, HEAD),
+        keys, keys_partner, values, values_partner,
+    )
+    done_0, done_2, done_13 = gather_z(done)
+
+    by_head, last_head = [], []
+    for k, block in enumerate((done_0, done_13[0], done_2, done_13[1])):
+        main = block[:half].reshape(depth, size, HEAD)
+        by_head.append(jnp.concatenate([main[j ^ k] for j in steps], axis=0))
+        last_head.append(block[half:])
+    attended = jnp.concatenate(by_head + [jnp.concatenate(last_head, axis=0)], axis=1)
+
+    def relative(value, axis):
+        parts = [
+            lax.dynamic_slice_in_dim(value, (z ^ k) * HEAD, HEAD, axis) for k in steps
+        ] + [lax.slice_in_dim(value, depth * HEAD, heads * HEAD, axis=axis)]
+        return jnp.concatenate(parts, axis=axis)
+
+    mix = relative(jnp.concatenate([mix_0, mix_13[0], mix_2, mix_13[1]], axis=0), 1)
+    attended_flipped = attended * mix
+    first = jnp.where(x == 0, out_t, out_partner)
+    second = jnp.where(x == 0, out_partner, out_t)
+    out_full = relative(jnp.concatenate([first, second], axis=1), 2)
+    partial = jnp.stack(
+        [dot32_t(attended, out_full[0]), dot32_t(attended_flipped, out_full[1])]
+    ).astype(bf)
+    partial = partial.reshape(2, depth, 2, 2, own_rows, 2 * slab)
+    core = u % 2
+    y = u // 2
+    keep = lax.dynamic_index_in_dim(partial, core, 3, keepdims=False)
+    send = lax.dynamic_index_in_dim(partial, 1 - core, 3, keepdims=False)
+    summed = keep.astype(jnp.float32) + swap_u(send, 1).astype(jnp.float32)
+    keep = lax.dynamic_index_in_dim(summed, y, 2, keepdims=False)
+    send = lax.dynamic_index_in_dim(summed, 1 - y, 2, keepdims=False).astype(bf)
+    summed = (keep + swap_u(send, 2).astype(jnp.float32)).astype(bf)
+    final = [summed[:, 0]] + [swap_z(summed[:, k], k) for k in steps if k]
+    placed = jnp.zeros((2, own_rows, depth, 2 * slab), bf)
+    for k in steps:
+        placed = lax.dynamic_update_slice_in_dim(placed, final[k][:, :, None], z ^ k, 2)
+    placed = placed.reshape(2, own_rows, width).astype(jnp.float32)
+    own_bits = lax.dynamic_slice_in_dim(out_bits, u * own_rows, own_rows, 0)
+    return (placed[0] + signed(own_bits) * placed[1]).astype(bf)
+
+
+def body(*arrays):
+    heads = arrays[2].shape[3] // HEAD
+    depth = lax.axis_size("blk") // 2
+    if depth == heads - 1 and depth == 4 and lax.axis_size("uly") == 4:
+        return stationary_plan(*arrays)
+    return gather_plan(*arrays)
 
 
 def solution(mesh):

time: 554 us -> 158 us (0.29)
  waiting for transfers between devices: 437 us -> 89.3 us
  blocking collectives: 82 us -> 9.7 us
  starting transfers between devices: 0.08 us -> 34.4 us
  matrix products: 14.4 us -> 1.4 us
  between operations: 13.3 us -> 0.55 us
  Pallas kernels: 0 us -> 11.9 us
    all_gather x2 -> x0, waiting for transfers between devices: 412 us -> none  [the longest x1 370 us: body(): lax.all_gather(qkv_weights, 'blk', axis=2, tiled=True)]
    ppermute x0 -> x29, waiting for transfers between devices: none -> 89.3 us  [the longest x20 77.2 us: swap_z(): lax.ppermute(value, 'blk', [(i, i ^ 2 * step) for i in range(groups)])]
    all_gather x3 -> x1, blocking collectives: 82 us -> 9.7 us  [stationary_plan(): rows = lax.all_gather(jnp.stack(held), 'uly', axis=0)]
    ppermute x0 -> x29, starting transfers between devices: none -> 34.4 us  [the longest x20 24.2 us: swap_z(): lax.ppermute(value, 'blk', [(i, i ^ 2 * step) for i in range(groups)])]
    unnamed x4 -> x0, waiting for transfers between devices: 25.9 us -> none
    dot_general x4 -> x2, matrix products: 14.4 us -> 1.4 us  [dot32_t(): lax.dot_general(a, b, (((1,), (1,)), ((), ())), preferred_element_type=jn...]
    pallas_call x0 -> x10, Pallas kernels: none -> 11.9 us  [the longest x3 7.53 us: project(): call(functools.partial(project_kernel, part, whole), [shape(3 * half if w...]
  transfers between devices with their start and end apart: 3 -> 29, of which waited for: 3 -> 18; matrix products, arithmetic and copies ran while one was open for 2% -> 1% of each run, Pallas kernels for 0% -> 7%
where the time goes in v2:
time: 158 us
  waiting for transfers between devices  89.3 us (57%)
  starting transfers between devices  34.4 us (22%)
  Pallas kernels  11.9 us (8%)
  blocking collectives  9.7 us (6%)
  local copies, waits for them, and re-layouts  7.95 us (5%)
  other arithmetic  2.92 us (2%)
    ppermute x20, waiting for transfers between devices, swap_z(): lax.ppermute(value, 'blk', [(i, i ^ 2 * step) for i in range(groups)])  77.2 us
    ppermute x20, starting transfers between devices, swap_z(): lax.ppermute(value, 'blk', [(i, i ^ 2 * step) for i in range(groups)])  24.2 us
    all_gather x1, blocking collectives, stationary_plan(): rows = lax.all_gather(jnp.stack(held), 'uly', axis=0)  9.7 us
    ppermute x7, starting transfers between devices, swap_x(): return lax.ppermute(value, 'blk', [(i, i ^ 1) for i in range(groups)])  9.57 us
    ppermute x2, waiting for transfers between devices, swap_u(): return lax.ppermute(value, 'uly', [(i, i ^ bit) for i in range(team)])  9.33 us
    pallas_call x3, Pallas kernels, project(): call(functools.partial(project_kernel, part, whole), [shape(3 * half if w...  7.53 us
    unnamed x28, local copies, waits for them, and re-layouts  4.92 us
  transfers between devices with their start and end apart: 29, of which 18 were waited for; matrix products, arithmetic and copies ran while one was open for 1% of the time, Pallas kernels for 7%

profile of v2, /device:TPU:0, one launch (start us, length us, event | category | flops | bytes accessed | tf_op | source)
XLA Modules:
  0.0 158.2 jit_solution(13522595702519581229)
XLA Ops:
  0.1 1.7 %copy-done = bf16[2,3,320,640]{3,2,1,0:T(8,128)(2,1)S(1)} copy-done((bf16[2,3,320,640]{3,2,1,0:T(8,128)(2,1)S(1)}, bf16[2,3,320,640]{3,2,1,0:T(8,128)(2,1)}, u32[]{:S(2)}) %copy-start) | copy-done | bytes 2457624
  1.8 1.1 copy-done.2
  2.9 0.9 copy-done.3
  3.8 0.9 copy-done.5
  4.7 1.1 shard_map.91
  5.8 3.0 %collective-permute-start.3 = (bf16[2,320,640]{2,1,0:T(8,128)(2,1)S(1)}, bf16[2,320,640]{2,1,0:T(8,128)(2,1)S(1)}, u32[]{:S(2)}, u32[]{:S(2)}) collective-permute-start(bf16[2,320,640]{2,1,0:T(8,128)(2,1)S(1)} %get-tuple-element.46), channel_id=1, source_target_pairs={{0,4},{4,0},{8,12},{12,8},{16,20},{20,16},{24,28},{28,24},{1,5},{5... | collective-permute-start | bytes 2457608 | tf_op jit(solution)/shard_map/ppermute | solution.py:305
  8.8 1.6 collective-permute-start
  10.4 2.6 %collective-permute-start.1 = (bf16[2,24,640]{2,1,0:T(8,128)(2,1)S(1)}, bf16[2,24,640]{2,1,0:T(8,128)(2,1)S(1)}, u32[]{:S(2)}, u32[]{:S(2)}) collective-permute-start(bf16[2,24,640]{2,1,0:T(8,128)(2,1)S(1)} %get-tuple-element.44), channel_id=1, source_target_pairs={{0,16},{4,20},{8,24},{12,28},{16,0},{20,4},{24,8},{28,12},{1,17},{... | collective-permute-start | bytes 184328 | tf_op jit(solution)/shard_map/ppermute | solution.py:308
  13.2 1.7 %collective-permute-start.4 = (bf16[96,640]{1,0:T(8,128)(2,1)S(1)}, bf16[96,640]{1,0:T(8,128)(2,1)S(1)}, u32[]{:S(2)}, u32[]{:S(2)}) collective-permute-start(bf16[96,640]{1,0:T(8,128)(2,1)S(1)} %get-tuple-element.47.sign_0), channel_id=1, source_target_pairs={{0,16},{4,20},{8,24},{12,28},{16,0},{20,4},{24,8},{28,12},{1,17},{... | collective-permute-start | bytes 368648 | tf_op jit(solution)/shard_map/ppermute | solution.py:308
  14.9 1.0 shard_map.94
  15.9 5.0 %collective-permute-done.1 = bf16[2,24,640]{2,1,0:T(8,128)(2,1)S(1)} collective-permute-done((bf16[2,24,640]{2,1,0:T(8,128)(2,1)S(1)}, bf16[2,24,640]{2,1,0:T(8,128)(2,1)S(1)}, u32[]{:S(2)}, u32[]{:S(2)}) %collective-permute-start.1) | collective-permute-done | bytes 61472 | tf_op jit(solution)/shard_map/ppermute | solution.py:308
  20.9 2.8 %collective-permute-done.4.sign_2 = bf16[96,640]{1,0:T(8,128)(2,1)S(1)} collective-permute-done((bf16[96,640]{1,0:T(8,128)(2,1)S(1)}, bf16[96,640]{1,0:T(8,128)(2,1)S(1)}, u32[]{:S(2)}, u32[]{:S(2)}) %collective-permute-start.4) | collective-permute-done | bytes 122912 | tf_op jit(solution)/shard_map/ppermute | solution.py:308
  23.8 9.7 %all-gather = bf16[16,2,24,640]{3,2,1,0:T(8,128)(2,1)S(1)} all-gather(bf16[4,2,24,640]{3,2,1,0:T(8,128)(2,1)S(1)} %pad_maximum_fusion.3), channel_id=2, replica_groups=mesh['blk'=8,'uly'=4] {'uly'}, dimensions={0}, use_global_device_ids=true | all-gather | bytes 1228800 | tf_op jit(solution)/shard_map/all_gather | solution.py:342
  34.2 3.0 %collective-permute-start.9 = (bf16[2,96,640]{2,1,0:T(8,128)(2,1)S(1)}, bf16[2,96,640]{2,1,0:T(8,128)(2,1)S(1)}, u32[]{:S(2)}, u32[]{:S(2)}) collective-permute-start(bf16[2,96,640]{2,1,0:T(8,128)(2,1)S(1)} %get-tuple-element.58), channel_id=1, source_target_pairs={{0,16},{4,20},{8,24},{12,28},{16,0},{20,4},{24,8},{28,12},{1,17},{... | collective-permute-start | bytes 737288 | tf_op jit(solution)/shard_map/ppermute | solution.py:308
  37.2 11.5 %collective-permute-done.9 = bf16[2,96,640]{2,1,0:T(8,128)(2,1)S(1)} collective-permute-done((bf16[2,96,640]{2,1,0:T(8,128)(2,1)S(1)}, bf16[2,96,640]{2,1,0:T(8,128)(2,1)S(1)}, u32[]{:S(2)}, u32[]{:S(2)}) %collective-permute-start.9) | collective-permute-done | bytes 245792 | tf_op jit(solution)/shard_map/ppermute | solution.py:308
  48.8 2.5 %shard_map.92 = (bf16[1152,128]{1,0:T(8,128)(2,1)S(1)}, f32[768,128]{1,0:T(8,128)S(1)}, f32[384,128]{1,0:T(8,128)S(1)}) custom-call(s32[2]{0:T(128)S(1)} %pad_add_fusion.place, bf16[2,384,640]{2,1,0:T(8,128)(2,1)S(1)} %bitcast.124, bf16[2,3,320,640]{3,2,1,0:T(8,128)(2,1)S(1)} %copy-done.1, ...), custom_call_target="tpu_custom_call" | custom-call | tf_op jit(solution)/shard_map/pallas_call | solution.py:359
  51.3 2.1 %collective-permute-start.6 = (bf16[1152,128]{1,0:T(8,128)(2,1)S(1)}, bf16[1152,128]{1,0:T(8,128)(2,1)S(1)}, u32[]{:S(2)}, u32[]{:S(2)}) collective-permute-start(bf16[1152,128]{1,0:T(8,128)(2,1)S(1)} %get-tuple-element.50), channel_id=1, source_target_pairs={{0,8},{4,12},{8,0},{12,4},{16,24},{20,28},{24,16},{28,20},{1,9},{5... | collective-permute-start | bytes 884744 | tf_op jit(solution)/shard_map/ppermute | solution.py:308
  53.4 0.7 collective-permute-done.8.partner_0.partner_1
  54.2 0.8 collective-permute-start.12
  55.0 12.8 %collective-permute-done.6.taken = bf16[1152,128]{1,0:T(8,128)(2,1)S(1)} collective-permute-done((bf16[1152,128]{1,0:T(8,128)(2,1)S(1)}, bf16[1152,128]{1,0:T(8,128)(2,1)S(1)}, u32[]{:S(2)}, u32[]{:S(2)}) %collective-permute-start.6) | collective-permute-done | bytes 294944 | tf_op jit(solution)/shard_map/ppermute | solution.py:308
  68.6 1.6 collective-permute-start.13
  70.2 8.3 %collective-permute-done.7 = bf16[768,128]{1,0:T(8,128)(2,1)S(1)} collective-permute-done((bf16[768,128]{1,0:T(8,128)(2,1)S(1)}, bf16[768,128]{1,0:T(8,128)(2,1)S(1)}, u32[]{:S(2)}, u32[]{:S(2)}) %collective-permute-start.7) | collective-permute-done | bytes 196640 | tf_op jit(solution)/shard_map/ppermute | solution.py:308
  78.5 2.5 %shard_map.95 = (bf16[1152,128]{1,0:T(8,128)(2,1)S(1)}, f32[768,128]{1,0:T(8,128)S(1)}, f32[384,128]{1,0:T(8,128)S(1)}) custom-call(s32[2]{0:T(128)S(1)} %pad_add_fusion.place, bf16[2,384,640]{2,1,0:T(8,128)(2,1)S(1)} %bitcast.125, bf16[2,3,320,640]{3,2,1,0:T(8,128)(2,1)S(1)} %copy-done.1, ...), custom_call_target="tpu_custom_call" | custom-call | tf_op jit(solution)/shard_map/pallas_call | solution.py:359
  81.1 8.9 %collective-permute-done.11.taken = bf16[1152,128]{1,0:T(8,128)(2,1)S(1)} collective-permute-done((bf16[1152,128]{1,0:T(8,128)(2,1)S(1)}, bf16[1152,128]{1,0:T(8,128)(2,1)S(1)}, u32[]{:S(2)}, u32[]{:S(2)}) %collective-permute-start.11) | collective-permute-done | bytes 294944 | tf_op jit(solution)/shard_map/ppermute | solution.py:308
  90.3 2.5 %shard_map.97 = (bf16[960,128]{1,0:T(8,128)(2,1)S(1)}, f32[480,128]{1,0:T(8,128)S(1)}, f32[480,128]{1,0:T(8,128)S(1)}) custom-call(s32[2]{0:T(128)S(1)} %pad_add_fusion.place, bf16[2,384,640]{2,1,0:T(8,128)(2,1)S(1)} %bitcast.126, bf16[2,3,320,640]{3,2,1,0:T(8,128)(2,1)S(1)} %copy-done.1, bf16[320,640]{1,0:T(8,128)(2,1)S(1)} %collective-permute-done.12.partner_0, ...), custom_call_target="tpu_custom_call" | custom-call | tf_op jit(solution)/shard_map/pallas_call | solution.py:359
  92.8 1.8 %collective-permute-start.14 = (bf16[960,128]{1,0:T(8,128)(2,1)S(1)}, bf16[960,128]{1,0:T(8,128)(2,1)S(1)}, u32[]{:S(2)}, u32[]{:S(2)}) collective-permute-start(bf16[960,128]{1,0:T(8,128)(2,1)S(1)} %get-tuple-element.71), channel_id=1, source_target_pairs={{0,8},{4,12},{8,0},{12,4},{16,24},{20,28},{24,16},{28,20},{1,9},{5... | collective-permute-start | bytes 737288 | tf_op jit(solution)/shard_map/ppermute | solution.py:308
  94.6 6.7 %collective-permute-done.16.taken = bf16[768,128]{1,0:T(8,128)(2,1)S(1)} collective-permute-done((bf16[768,128]{1,0:T(8,128)(2,1)S(1)}, bf16[768,128]{1,0:T(8,128)(2,1)S(1)}, u32[]{:S(2)}, u32[]{:S(2)}) %collective-permute-start.16) | collective-permute-done | bytes 196640 | tf_op jit(solution)/shard_map/ppermute | solution.py:308
  101.3 0.7 shard_map.99.keys_a
  102.1 1.6 collective-permute-start.18
  104.3 2.9 %collective-permute-start.15 = (bf16[480,128]{1,0:T(8,128)(2,1)S(1)}, bf16[480,128]{1,0:T(8,128)(2,1)S(1)}, u32[]{:S(2)}, u32[]{:S(2)}) collective-permute-start(bf16[480,128]{1,0:T(8,128)(2,1)S(1)} %get-tuple-element.73), channel_id=1, source_target_pairs={{0,16},{4,20},{8,24},{12,28},{16,0},{20,4},{24,8},{28,12},{1,17},{... | collective-permute-start | bytes 368648 | tf_op jit(solution)/shard_map/ppermute | solution.py:308
  107.2 1.5 collective-permute-start.21
  108.7 3.3 %collective-permute-done.22 = bf16[96,640]{1,0:T(8,128)(2,1)S(1)} collective-permute-done((bf16[96,640]{1,0:T(8,128)(2,1)S(1)}, bf16[96,640]{1,0:T(8,128)(2,1)S(1)}, u32[]{:S(2)}, u32[]{:S(2)}) %collective-permute-start.22) | collective-permute-done | bytes 122912 | tf_op jit(solution)/shard_map/ppermute | solution.py:308
  112.1 2.0 %collective-permute-done.17.keys_b = bf16[768,128]{1,0:T(8,128)(2,1)S(1)} collective-permute-done((bf16[768,128]{1,0:T(8,128)(2,1)S(1)}, bf16[768,128]{1,0:T(8,128)(2,1)S(1)}, u32[]{:S(2)}, u32[]{:S(2)}) %collective-permute-start.17) | collective-permute-done | bytes 196640 | tf_op jit(solution)/shard_map/ppermute | solution.py:305
  114.6 1.4 shard_map.100
  116.0 2.6 %collective-permute-start.19 = (bf16[480,128]{1,0:T(8,128)(2,1)S(1)}, bf16[480,128]{1,0:T(8,128)(2,1)S(1)}, u32[]{:S(2)}, u32[]{:S(2)}) collective-permute-start(bf16[480,128]{1,0:T(8,128)(2,1)S(1)} %shard_map.100), channel_id=1, source_target_pairs={{0,16},{4,20},{8,24},{12,28},{16,0},{20,4},{24,8},{28,12},{1,17},{... | collective-permute-start | bytes 368648 | tf_op jit(solution)/shard_map/ppermute | solution.py:308
  118.6 2.1 %collective-permute-done.23 = bf16[2,96,640]{2,1,0:T(8,128)(2,1)S(1)} collective-permute-done((bf16[2,96,640]{2,1,0:T(8,128)(2,1)S(1)}, bf16[2,96,640]{2,1,0:T(8,128)(2,1)S(1)}, u32[]{:S(2)}, u32[]{:S(2)}) %collective-permute-start.23) | collective-permute-done | bytes 245792 | tf_op jit(solution)/shard_map/ppermute | solution.py:308
  121.0 3.9 %collective-permute-done.19 = bf16[480,128]{1,0:T(8,128)(2,1)S(1)} collective-permute-done((bf16[480,128]{1,0:T(8,128)(2,1)S(1)}, bf16[480,128]{1,0:T(8,128)(2,1)S(1)}, u32[]{:S(2)}, u32[]{:S(2)}) %collective-permute-start.19) | collective-permute-done | bytes 122912 | tf_op jit(solution)/shard_map/ppermute | solution.py:308
  125.0 7.2 %collective-permute-done.20 = bf16[2,480,128]{2,1,0:T(8,128)(2,1)S(1)} collective-permute-done((bf16[2,480,128]{2,1,0:T(8,128)(2,1)S(1)}, bf16[2,480,128]{2,1,0:T(8,128)(2,1)S(1)}, u32[]{:S(2)}, u32[]{:S(2)}) %collective-permute-start.20) | collective-permute-done | bytes 245792 | tf_op jit(solution)/shard_map/ppermute | solution.py:308
  133.2 0.7 fusion
  133.9 0.7 fusion.1
  134.8 1.8 %collective-permute-done.24 = bf16[2,4,2,24,640]{4,3,2,1,0:T(8,128)(2,1)S(1)} collective-permute-done((bf16[2,4,2,24,640]{4,3,2,1,0:T(8,128)(2,1)S(1)}, bf16[2,4,2,24,640]{4,3,2,1,0:T(8,128)(2,1)S(1)}, u32[]{:S(2)}, u32[]{:S(2)}) %collective-permute-start.24) | collective-permute-done | bytes 491552 | tf_op jit(solution)/shard_map/ppermute | solution.py:311
  137.3 7.5 %collective-permute-done.25 = bf16[2,4,24,640]{3,2,1,0:T(8,128)(2,1)S(1)} collective-permute-done((bf16[2,4,24,640]{3,2,1,0:T(8,128)(2,1)S(1)}, bf16[2,4,24,640]{3,2,1,0:T(8,128)(2,1)S(1)}, u32[]{:S(2)}, u32[]{:S(2)}) %collective-permute-start.25) | collective-permute-done | bytes 245792 | tf_op jit(solution)/shard_map/ppermute | solution.py:311
  145.3 2.8 %collective-permute-start.27 = (bf16[2,24,640]{2,1,0:T(8,128)(2,1)S(1)}, bf16[2,24,640]{2,1,0:T(8,128)(2,1)S(1)}, u32[]{:S(2)}, u32[]{:S(2)}) collective-permute-start(bf16[2,24,640]{2,1,0:T(8,128)(2,1)S(1)} %get-tuple-element.91), channel_id=1, source_target_pairs={{0,16},{4,20},{8,24},{12,28},{16,0},{20,4},{24,8},{28,12},{1,17},{... | collective-permute-start | bytes 184328 | tf_op jit(solution)/shard_map/ppermute | solution.py:308
  148.0 1.3 collective-permute-start.28
  149.4 1.5 collective-permute-done.27
  151.1 3.0 %collective-permute-done.28 = bf16[2,24,640]{2,1,0:T(8,128)(2,1)S(1)} collective-permute-done((bf16[2,24,640]{2,1,0:T(8,128)(2,1)S(1)}, bf16[2,24,640]{2,1,0:T(8,128)(2,1)S(1)}, u32[]{:S(2)}, u32[]{:S(2)}) %collective-permute-start.28) | collective-permute-done | bytes 61472 | tf_op jit(solution)/shard_map/ppermute | solution.py:308
  154.1 2.3 %dynamic_update_slice.15 = bf16[2,24,4,640]{3,2,1,0:T(4,128)(2,1)S(1)} dynamic-update-slice(bf16[2,24,4,640]{3,2,1,0:T(4,128)(2,1)S(1)} %copy.14, bf16[2,24,1,640]{3,2,1,0:T(2,128)(2,1)S(1)} %copy.15, s32[]{:T(128)} %constant.67.clone.1, s32[]{:T(128)} %constant.67.clone.1, s32[]{:T(128)S(6)} %select_n.93, s32[]{:T(128)} %constant.67.clone.1) | dynamic-update-slice | bytes 122884 | tf_op jit(solution)/shard_map/dynamic_update_slice | solution.py:440
  156.5 1.7 %add_convert_fusion.1 = bf16[24,2560]{1,0:T(8,128)(2,1)} fusion(f32[24,2560]{1,0:T(8,128)S(1)} %bitcast.138, f32[24,2560]{1,0:T(8,128)S(1)} %bitcast.139, s32[96,2560]{1,0:T(8,128)} %param.17, s32[]{:T(128)S(6)} %select_n.94), kind=kLoop, calls=%fused_computation.49 | loop fusion | flops 368640 | bytes 860164 | tf_op jit(solution)/shard_map/convert_element_type | solution.py:443
  (95 shorter events, 6.6 us)
Async XLA Ops:
  0.1 1.7 %copy-start = (bf16[2,3,320,640]{3,2,1,0:T(8,128)(2,1)S(1)}, bf16[2,3,320,640]{3,2,1,0:T(8,128)(2,1)}, u32[]{:S(2)}) copy-start(bf16[2,3,320,640]{3,2,1,0:T(8,128)(2,1)} %weights.9) | copy-start | bytes 7372804
  1.8 1.1 copy-start.2
  2.9 0.9 copy-start.3
  3.8 0.9 copy-start.5
  4.7 10.2 %copy-start.1 = (bf16[2,3,320,640]{3,2,1,0:T(8,128)(2,1)S(1)}, bf16[2,3,320,640]{3,2,1,0:T(8,128)(2,1)}, u32[]{:S(2)}) copy-start(bf16[2,3,320,640]{3,2,1,0:T(8,128)(2,1)} %weights.9) | copy-start | bytes 7372804
  4.7 10.2 %copy-start.4 = (s32[96,640]{1,0:T(8,128)S(1)}, s32[96,640]{1,0:T(8,128)}, u32[]{:S(2)}) copy-start(s32[96,640]{1,0:T(8,128)} %mix_bits.1) | copy-start | bytes 737284
  5.8 27.8 %collective-permute-start.3 = (bf16[2,320,640]{2,1,0:T(8,128)(2,1)S(1)}, bf16[2,320,640]{2,1,0:T(8,128)(2,1)S(1)}, u32[]{:S(2)}, u32[]{:S(2)}) collective-permute-start(bf16[2,320,640]{2,1,0:T(8,128)(2,1)S(1)} %get-tuple-element.46), channel_id=1, source_target_pairs={{0,4},{4,0},{8,12},{12,8},{16,20},{20,16},{24,28},{28,24},{1,5},{5... | collective-permute-start | bytes 2457608 | tf_op jit(solution)/shard_map/ppermute | solution.py:305
  8.8 7.1 %collective-permute-start = (bf16[2,24,640]{2,1,0:T(8,128)(2,1)S(1)}, bf16[2,24,640]{2,1,0:T(8,128)(2,1)S(1)}, u32[]{:S(2)}, u32[]{:S(2)}) collective-permute-start(bf16[2,24,640]{2,1,0:T(8,128)(2,1)S(1)} %get-tuple-element.43), channel_id=1, source_target_pairs={{0,8},{4,12},{8,0},{12,4},{16,24},{20,28},{24,16},{28,20},{1,9},{5... | collective-permute-start | bytes 184328 | tf_op jit(solution)/shard_map/ppermute | solution.py:308
  10.4 10.5 %collective-permute-start.1 = (bf16[2,24,640]{2,1,0:T(8,128)(2,1)S(1)}, bf16[2,24,640]{2,1,0:T(8,128)(2,1)S(1)}, u32[]{:S(2)}, u32[]{:S(2)}) collective-permute-start(bf16[2,24,640]{2,1,0:T(8,128)(2,1)S(1)} %get-tuple-element.44), channel_id=1, source_target_pairs={{0,16},{4,20},{8,24},{12,28},{16,0},{20,4},{24,8},{28,12},{1,17},{... | collective-permute-start | bytes 184328 | tf_op jit(solution)/shard_map/ppermute | solution.py:308
  13.0 7.9 %collective-permute-start.2 = (bf16[2,24,640]{2,1,0:T(8,128)(2,1)S(1)}, bf16[2,24,640]{2,1,0:T(8,128)(2,1)S(1)}, u32[]{:S(2)}, u32[]{:S(2)}) collective-permute-start(bf16[2,24,640]{2,1,0:T(8,128)(2,1)S(1)} %get-tuple-element.45), channel_id=1, source_target_pairs={{0,24},{4,28},{8,16},{12,20},{16,8},{20,12},{24,0},{28,4},{1,25},{... | collective-permute-start | bytes 184328 | tf_op jit(solution)/shard_map/ppermute | solution.py:308
  13.2 10.5 %collective-permute-start.4 = (bf16[96,640]{1,0:T(8,128)(2,1)S(1)}, bf16[96,640]{1,0:T(8,128)(2,1)S(1)}, u32[]{:S(2)}, u32[]{:S(2)}) collective-permute-start(bf16[96,640]{1,0:T(8,128)(2,1)S(1)} %get-tuple-element.47.sign_0), channel_id=1, source_target_pairs={{0,16},{4,20},{8,24},{12,28},{16,0},{20,4},{24,8},{28,12},{1,17},{... | collective-permute-start | bytes 368648 | tf_op jit(solution)/shard_map/ppermute | solution.py:308
  23.7 10.5 %collective-permute-start.5 = (bf16[2,96,640]{2,1,0:T(8,128)(2,1)S(1)}, bf16[2,96,640]{2,1,0:T(8,128)(2,1)S(1)}, u32[]{:S(2)}, u32[]{:S(2)}) collective-permute-start(bf16[2,96,640]{2,1,0:T(8,128)(2,1)S(1)} %pad_maximum_fusion.4), channel_id=1, source_target_pairs={{0,8},{4,12},{8,0},{12,4},{16,24},{20,28},{24,16},{28,20},{1,9},{5... | collective-permute-start | bytes 737288 | tf_op jit(solution)/shard_map/ppermute | solution.py:308
  33.6 20.6 %collective-permute-start.8 = (bf16[2,320,640]{2,1,0:T(8,128)(2,1)S(1)}, bf16[2,320,640]{2,1,0:T(8,128)(2,1)S(1)}, u32[]{:S(2)}, u32[]{:S(2)}) collective-permute-start(bf16[2,320,640]{2,1,0:T(8,128)(2,1)S(1)} %get-tuple-element.56), channel_id=1, source_target_pairs={{0,4},{4,0},{8,12},{12,8},{16,20},{20,16},{24,28},{28,24},{1,5},{5... | collective-permute-start | bytes 2457608 | tf_op jit(solution)/shard_map/ppermute | solution.py:305
  34.2 14.5 %collective-permute-start.9 = (bf16[2,96,640]{2,1,0:T(8,128)(2,1)S(1)}, bf16[2,96,640]{2,1,0:T(8,128)(2,1)S(1)}, u32[]{:S(2)}, u32[]{:S(2)}) collective-permute-start(bf16[2,96,640]{2,1,0:T(8,128)(2,1)S(1)} %get-tuple-element.58), channel_id=1, source_target_pairs={{0,16},{4,20},{8,24},{12,28},{16,0},{20,4},{24,8},{28,12},{1,17},{... | collective-permute-start | bytes 737288 | tf_op jit(solution)/shard_map/ppermute | solution.py:308
  48.7 19.8 %collective-permute-start.10 = (bf16[2,2,96,640]{3,2,0,1:T(8,128)(2,1)S(1)}, bf16[2,2,96,640]{3,2,0,1:T(8,128)(2,1)S(1)}, u32[]{:S(2)}, u32[]{:S(2)}) collective-permute-start(bf16[2,2,96,640]{3,2,0,1:T(8,128)(2,1)S(1)} %pad_maximum_fusion), channel_id=1, source_target_pairs={{0,8},{4,12},{8,0},{12,4},{16,24},{20,28},{24,16},{28,20},{1,9},{5... | collective-permute-start | bytes 1474568 | tf_op jit(solution)/shard_map/ppermute | solution.py:308
  51.3 16.5 %collective-permute-start.6 = (bf16[1152,128]{1,0:T(8,128)(2,1)S(1)}, bf16[1152,128]{1,0:T(8,128)(2,1)S(1)}, u32[]{:S(2)}, u32[]{:S(2)}) collective-permute-start(bf16[1152,128]{1,0:T(8,128)(2,1)S(1)} %get-tuple-element.50), channel_id=1, source_target_pairs={{0,8},{4,12},{8,0},{12,4},{16,24},{20,28},{24,16},{28,20},{1,9},{5... | collective-permute-start | bytes 884744 | tf_op jit(solution)/shard_map/ppermute | solution.py:308
  54.2 14.4 %collective-permute-start.12 = (bf16[320,640]{1,0:T(8,128)(2,1)S(1)}, bf16[320,640]{1,0:T(8,128)(2,1)S(1)}, u32[]{:S(2)}, u32[]{:S(2)}) collective-permute-start(bf16[320,640]{1,0:T(8,128)(2,1)S(1)} %get-tuple-element.63), channel_id=1, source_target_pairs={{0,4},{4,0},{8,12},{12,8},{16,20},{20,16},{24,28},{28,24},{1,5},{5... | collective-permute-start | bytes 1228808 | tf_op jit(solution)/shard_map/ppermute | solution.py:305
  67.9 10.6 %collective-permute-start.7 = (bf16[768,128]{1,0:T(8,128)(2,1)S(1)}, bf16[768,128]{1,0:T(8,128)(2,1)S(1)}, u32[]{:S(2)}, u32[]{:S(2)}) collective-permute-start(bf16[768,128]{1,0:T(8,128)(2,1)S(1)} %get-tuple-element.52), channel_id=1, source_target_pairs={{0,16},{4,20},{8,24},{12,28},{16,0},{20,4},{24,8},{28,12},{1,17},{... | collective-permute-start | bytes 589832 | tf_op jit(solution)/shard_map/ppermute | solution.py:308
  68.6 21.7 %collective-permute-start.13 = (bf16[320,640]{1,0:T(8,128)(2,1)S(1)}, bf16[320,640]{1,0:T(8,128)(2,1)S(1)}, u32[]{:S(2)}, u32[]{:S(2)}) collective-permute-start(bf16[320,640]{1,0:T(8,128)(2,1)S(1)} %get-tuple-element.68), channel_id=1, source_target_pairs={{0,4},{4,0},{8,12},{12,8},{16,20},{20,16},{24,28},{28,24},{1,5},{5... | collective-permute-start | bytes 1228808 | tf_op jit(solution)/shard_map/ppermute | solution.py:305
  81.1 9.0 %collective-permute-start.11 = (bf16[1152,128]{1,0:T(8,128)(2,1)S(1)}, bf16[1152,128]{1,0:T(8,128)(2,1)S(1)}, u32[]{:S(2)}, u32[]{:S(2)}) collective-permute-start(bf16[1152,128]{1,0:T(8,128)(2,1)S(1)} %get-tuple-element.61), channel_id=1, source_target_pairs={{0,8},{4,12},{8,0},{12,4},{16,24},{20,28},{24,16},{28,20},{1,9},{5... | collective-permute-start | bytes 884744 | tf_op jit(solution)/shard_map/ppermute | solution.py:308
  90.1 11.2 %collective-permute-start.16 = (bf16[768,128]{1,0:T(8,128)(2,1)S(1)}, bf16[768,128]{1,0:T(8,128)(2,1)S(1)}, u32[]{:S(2)}, u32[]{:S(2)}) collective-permute-start(bf16[768,128]{1,0:T(8,128)(2,1)S(1)} %get-tuple-element.74), channel_id=1, source_target_pairs={{0,16},{4,20},{8,24},{12,28},{16,0},{20,4},{24,8},{28,12},{1,17},{... | collective-permute-start | bytes 589832 | tf_op jit(solution)/shard_map/ppermute | solution.py:308
  90.3 11.0 %copy-start.6 = (f32[640]{0:T(1024)S(1)}, f32[640]{0:T(1024)}, u32[]{:S(2)}) copy-start(f32[640]{0:T(1024)} %param.14) | copy-start | bytes 7684
  90.3 16.9 %copy-start.8 = (bf16[2,640,320]{1,2,0:T(8,128)(2,1)S(1)}, bf16[2,640,320]{1,2,0:T(8,128)(2,1)}, u32[]{:S(2)}) copy-start(bf16[2,640,320]{1,2,0:T(8,128)(2,1)} %param.15) | copy-start | bytes 2457604
  92.8 21.8 %copy-start.7 = (f32[640]{0:T(1024)S(1)}, f32[640]{0:T(1024)}, u32[]{:S(2)}) copy-start(f32[640]{0:T(1024)} %param.13) | copy-start | bytes 7684
  92.8 11.4 %collective-permute-start.14 = (bf16[960,128]{1,0:T(8,128)(2,1)S(1)}, bf16[960,128]{1,0:T(8,128)(2,1)S(1)}, u32[]{:S(2)}, u32[]{:S(2)}) collective-permute-start(bf16[960,128]{1,0:T(8,128)(2,1)S(1)} %get-tuple-element.71), channel_id=1, source_target_pairs={{0,8},{4,12},{8,0},{12,4},{16,24},{20,28},{24,16},{28,20},{1,9},{5... | collective-permute-start | bytes 737288 | tf_op jit(solution)/shard_map/ppermute | solution.py:308
  102.0 10.0 %collective-permute-start.22 = (bf16[96,640]{1,0:T(8,128)(2,1)S(1)}, bf16[96,640]{1,0:T(8,128)(2,1)S(1)}, u32[]{:S(2)}, u32[]{:S(2)}) collective-permute-start(bf16[96,640]{1,0:T(8,128)(2,1)S(1)} %get-tuple-element.78), channel_id=1, source_target_pairs={{0,16},{4,20},{8,24},{12,28},{16,0},{20,4},{24,8},{28,12},{1,17},{... | collective-permute-start | bytes 368648 | tf_op jit(solution)/shard_map/ppermute | solution.py:308
  102.1 10.0 %collective-permute-start.18 = (bf16[768,128]{1,0:T(8,128)(2,1)S(1)}, bf16[768,128]{1,0:T(8,128)(2,1)S(1)}, u32[]{:S(2)}, u32[]{:S(2)}) collective-permute-start(bf16[768,128]{1,0:T(8,128)(2,1)S(1)} %add_convert_fusion.values_a), channel_id=1, source_target_pairs={{0,4},{4,0},{8,12},{12,8},{16,20},{20,16},{24,28},{28,24},{1,5},{5... | collective-permute-start | bytes 589832 | tf_op jit(solution)/shard_map/ppermute | solution.py:305
  103.7 10.5 %collective-permute-start.17 = (bf16[768,128]{1,0:T(8,128)(2,1)S(1)}, bf16[768,128]{1,0:T(8,128)(2,1)S(1)}, u32[]{:S(2)}, u32[]{:S(2)}) collective-permute-start(bf16[768,128]{1,0:T(8,128)(2,1)S(1)} %shard_map.99.keys_a), channel_id=1, source_target_pairs={{0,4},{4,0},{8,12},{12,8},{16,20},{20,16},{24,28},{28,24},{1,5},{5... | collective-permute-start | bytes 589832 | tf_op jit(solution)/shard_map/ppermute | solution.py:305
  104.3 10.3 %collective-permute-start.15 = (bf16[480,128]{1,0:T(8,128)(2,1)S(1)}, bf16[480,128]{1,0:T(8,128)(2,1)S(1)}, u32[]{:S(2)}, u32[]{:S(2)}) collective-permute-start(bf16[480,128]{1,0:T(8,128)(2,1)S(1)} %get-tuple-element.73), channel_id=1, source_target_pairs={{0,16},{4,20},{8,24},{12,28},{16,0},{20,4},{24,8},{28,12},{1,17},{... | collective-permute-start | bytes 368648 | tf_op jit(solution)/shard_map/ppermute | solution.py:308
  107.2 25.4 %collective-permute-start.21 = (bf16[2,320,640]{2,1,0:T(8,128)(2,1)S(1)}, bf16[2,320,640]{2,1,0:T(8,128)(2,1)S(1)}, u32[]{:S(2)}, u32[]{:S(2)}) collective-permute-start(bf16[2,320,640]{2,1,0:T(8,128)(2,1)S(1)} %bitcast.143), channel_id=1, source_target_pairs={{0,4},{4,0},{8,12},{12,8},{16,20},{20,16},{24,28},{28,24},{1,5},{5... | collective-permute-start | bytes 2457608 | tf_op jit(solution)/shard_map/ppermute | solution.py:305
  112.1 8.6 %collective-permute-start.23 = (bf16[2,96,640]{2,1,0:T(8,128)(2,1)S(1)}, bf16[2,96,640]{2,1,0:T(8,128)(2,1)S(1)}, u32[]{:S(2)}, u32[]{:S(2)}) collective-permute-start(bf16[2,96,640]{2,1,0:T(8,128)(2,1)S(1)} %pad_maximum_fusion.6), channel_id=1, source_target_pairs={{0,8},{4,12},{8,0},{12,4},{16,24},{20,28},{24,16},{28,20},{1,9},{5... | collective-permute-start | bytes 737288 | tf_op jit(solution)/shard_map/ppermute | solution.py:308
  116.0 8.8 %collective-permute-start.19 = (bf16[480,128]{1,0:T(8,128)(2,1)S(1)}, bf16[480,128]{1,0:T(8,128)(2,1)S(1)}, u32[]{:S(2)}, u32[]{:S(2)}) collective-permute-start(bf16[480,128]{1,0:T(8,128)(2,1)S(1)} %shard_map.100), channel_id=1, source_target_pairs={{0,16},{4,20},{8,24},{12,28},{16,0},{20,4},{24,8},{28,12},{1,17},{... | collective-permute-start | bytes 368648 | tf_op jit(solution)/shard_map/ppermute | solution.py:308
  124.9 7.3 %collective-permute-start.20 = (bf16[2,480,128]{2,1,0:T(8,128)(2,1)S(1)}, bf16[2,480,128]{2,1,0:T(8,128)(2,1)S(1)}, u32[]{:S(2)}, u32[]{:S(2)}) collective-permute-start(bf16[2,480,128]{2,1,0:T(8,128)(2,1)S(1)} %pad_maximum_fusion.5), channel_id=1, source_target_pairs={{0,8},{4,12},{8,0},{12,4},{16,24},{20,28},{24,16},{28,20},{1,9},{5... | collective-permute-start | bytes 737288 | tf_op jit(solution)/shard_map/ppermute | solution.py:308
  134.7 1.9 %collective-permute-start.24 = (bf16[2,4,2,24,640]{4,3,2,1,0:T(8,128)(2,1)S(1)}, bf16[2,4,2,24,640]{4,3,2,1,0:T(8,128)(2,1)S(1)}, u32[]{:S(2)}, u32[]{:S(2)}) collective-permute-start(bf16[2,4,2,24,640]{4,3,2,1,0:T(8,128)(2,1)S(1)} %fusion.3), channel_id=1, source_target_pairs={{0,1},{1,0},{2,3},{3,2},{4,5},{5,4},{6,7},{7,6},{8,9},{9,8},{10,11... | collective-permute-start | bytes 1474568 | tf_op jit(solution)/shard_map/ppermute | solution.py:311
  136.8 8.1 %collective-permute-start.25 = (bf16[2,4,24,640]{3,2,1,0:T(8,128)(2,1)S(1)}, bf16[2,4,24,640]{3,2,1,0:T(8,128)(2,1)S(1)}, u32[]{:S(2)}, u32[]{:S(2)}) collective-permute-start(bf16[2,4,24,640]{3,2,1,0:T(8,128)(2,1)S(1)} %fusion.17), channel_id=1, source_target_pairs={{0,2},{1,3},{2,0},{3,1},{4,6},{5,7},{6,4},{7,5},{8,10},{9,11},{10,... | collective-permute-start | bytes 737288 | tf_op jit(solution)/shard_map/ppermute | solution.py:311
  144.9 4.5 %collective-permute-start.26 = (bf16[2,24,640]{2,1,0:T(8,128)(2,1)S(1)}, bf16[2,24,640]{2,1,0:T(8,128)(2,1)S(1)}, u32[]{:S(2)}, u32[]{:S(2)}) collective-permute-start(bf16[2,24,640]{2,1,0:T(8,128)(2,1)S(1)} %get-tuple-element.92), channel_id=1, source_target_pairs={{0,8},{4,12},{8,0},{12,4},{16,24},{20,28},{24,16},{28,20},{1,9},{5... | collective-permute-start | bytes 184328 | tf_op jit(solution)/shard_map/ppermute | solution.py:308
  145.3 5.7 %collective-permute-start.27 = (bf16[2,24,640]{2,1,0:T(8,128)(2,1)S(1)}, bf16[2,24,640]{2,1,0:T(8,128)(2,1)S(1)}, u32[]{:S(2)}, u32[]{:S(2)}) collective-permute-start(bf16[2,24,640]{2,1,0:T(8,128)(2,1)S(1)} %get-tuple-element.91), channel_id=1, source_target_pairs={{0,16},{4,20},{8,24},{12,28},{16,0},{20,4},{24,8},{28,12},{1,17},{... | collective-permute-start | bytes 184328 | tf_op jit(solution)/shard_map/ppermute | solution.py:308
  148.0 6.0 %collective-permute-start.28 = (bf16[2,24,640]{2,1,0:T(8,128)(2,1)S(1)}, bf16[2,24,640]{2,1,0:T(8,128)(2,1)S(1)}, u32[]{:S(2)}, u32[]{:S(2)}) collective-permute-start(bf16[2,24,640]{2,1,0:T(8,128)(2,1)S(1)} %get-tuple-element.90), channel_id=1, source_target_pairs={{0,24},{4,28},{8,16},{12,20},{16,8},{20,12},{24,0},{28,4},{1,25},{... | collective-permute-start | bytes 184328 | tf_op jit(solution)/shard_map/ppermute | solution.py:308
